TPU v7x, 32 devices: a whole 2x2x4 slice. The times are simulated.
32 devices in a mesh: section: 2 (over y), dp: 16 (over z, x, core).
Axes of the slice: x: 2, y: 2, z: 4, core: 2. Of those that a mesh axis runs over, the one named last changes fastest.
Arguments:
- token_rows: bfloat16 [2, 8192, 512], P('section', 'dp'), may hold values from -6 to 6
- lengths: int32 [16, 2, 8], P('dp'), may hold values from 1 to 100, 512 in all within a row
- self_qkv: bfloat16 [2, 512, 1536], P('section'), may hold values from -0.25 to 0.25
- self_out: bfloat16 [2, 512, 512], P('section'), may hold values from -1 to 1
- ffn_in: bfloat16 [2, 512, 2048], P('section'), may hold values from -0.25 to 0.25
- ffn_in_bias: bfloat16 [2, 2048], P('section'), may hold values from -3 to 3
- ffn_out: bfloat16 [2, 2048, 512], P('section'), may hold values from -0.125 to 0.125
- ffn_out_bias: bfloat16 [2, 512], P('section'), may hold values from -3 to 3
- norm_gain: bfloat16 [2, 2, 512], P('section'), may hold values from 0.25 to 1.75
- norm_bias: bfloat16 [2, 2, 512], P('section'), may hold values from -3 to 3
- cross_weights: bfloat16 [2, 512, 1024], P('section')
- cross_gain: bfloat16 [512], replicated, may hold values from 0.25 to 1.75
- cross_bias: bfloat16 [512], replicated, may hold values from -3 to 3
- output_grad: bfloat16 [8192, 512], P('dp'), may hold values from -6 to 6
Outputs:
- layer_rows: bfloat16 [2, 8192, 512], P('section', 'dp')
- rows_grad: float32 [2, 8192, 512], P('section', 'dp')
- self_qkv_grad: float32 [2, 512, 1536], P('section')
- self_out_grad: float32 [2, 512, 512], P('section')
- ffn_in_grad: float32 [2, 512, 2048], P('section')
- ffn_in_bias_grad: float32 [2, 2048], P('section')
- ffn_out_grad: float32 [2, 2048, 512], P('section')
- ffn_out_bias_grad: float32 [2, 512], P('section')
- norm_gain_grad: float32 [2, 2, 512], P('section')
- norm_bias_grad: float32 [2, 2, 512], P('section')
- cross_weights_grad: float32 [2, 512, 1024], P('section')
- cross_gain_grad: float32 [512], replicated
- cross_bias_grad: float32 [512], replicated
Inputs may be any that keep to these rules, and one draw needn't show every extreme that they name: Each packed row has 8 source and 8 target sentences; source sentence j and target sentence j form a pair; each side's lengths sum to 512 and the longest is 100.
All inputs are finite; a program needn't handle non-finite values.
Results may differ from a plain program's by a relative error of at most 0.02.
Values may be sent and summed in bfloat16 or wider, within the bound.
No kernel may reach another device: no remote copies, remote signals or barrier semaphores. Data moves between devices by JAX's collectives and lax.ppermute only.
A program may use at most 192 MiB of HBM per device.

v0:
```python
import jax
import jax.numpy as jnp
from jax import lax
from jax.sharding import PartitionSpec as P

D = 512
HEADS = 8
HEAD_DIM = 64
REPEATS = 2


EPSILON = 1e-05
MASKED = -1000000000.0


def from_behind(shard, axis, by):
    size = lax.axis_size(axis)
    pairs = [(i, i + by) for i in range(size) if 0 <= i + by < size]
    return lax.ppermute(shard, axis, pairs)


def product(former, latter):
    return jnp.dot(former, latter, preferred_element_type=jnp.float32)


def left_transposed(former, latter):
    return lax.dot_general(
        former, latter, (((0,), (0,)), ((), ())), preferred_element_type=jnp.float32
    )


def right_transposed(former, latter):
    return lax.dot_general(
        former, latter, (((1,), (1,)), ((), ())), preferred_element_type=jnp.float32
    )


def layer_norm(values, norm_gain, norm_offset):
    centre = values - jnp.mean(values, axis=-1, keepdims=True)
    spread = jnp.mean(centre * centre, axis=-1, keepdims=True)
    return centre * lax.rsqrt(spread + EPSILON) * norm_gain + norm_offset


def norm_backward(values, norm_gain, norm_offset, grad_out):
    result, pull_back = jax.vjp(layer_norm, values, norm_gain, norm_offset)
    return pull_back(grad_out)


def split_heads(matrix, blocks):
    return matrix.reshape(blocks, -1, HEADS, HEAD_DIM)


def segment_ids(length_rows, row_len):
    bounds = jnp.cumsum(length_rows, axis=-1)
    places = jnp.arange(row_len, dtype=jnp.int32)
    return jnp.sum((places[None, :, None] >= bounds[:, None, :]).astype(jnp.int32), axis=-1)


def attend(queries, key_rows, values, allowed):
    blocks = allowed.shape[0]
    scaling = HEAD_DIM ** (-0.5)
    scores = (
        jnp.einsum(
            "rqhd,rkhd->rhqk",
            split_heads(queries, blocks),
            split_heads(key_rows, blocks),
            preferred_element_type=jnp.float32,
        )
        * scaling
    )
    scores = jnp.where(allowed[:, None], scores, MASKED)
    highest = jnp.max(scores, axis=-1, keepdims=True)
    powered = jnp.exp(scores - highest)
    totals = jnp.sum(powered, axis=-1, keepdims=True)
    attn_probs = (powered / totals).astype(jnp.bfloat16)
    attended = jnp.einsum(
        "rhqk,rkhd->rqhd",
        attn_probs,
        split_heads(values, blocks),
        preferred_element_type=jnp.float32,
    )
    return (attended.reshape(queries.shape[0], D).astype(jnp.bfloat16), highest + jnp.log(totals))


def attend_backward(queries, key_rows, values, allowed, log_totals, grad_attended):
    blocks = allowed.shape[0]
    scaling = HEAD_DIM ** (-0.5)
    query_heads = split_heads(queries, blocks)
    key_heads = split_heads(key_rows, blocks)
    value_heads = split_heads(values, blocks)
    grad_heads = split_heads(grad_attended, blocks)
    scores = (
        jnp.einsum("rqhd,rkhd->rhqk", query_heads, key_heads, preferred_element_type=jnp.float32)
        * scaling
    )
    scores = jnp.where(allowed[:, None], scores, MASKED)
    attn_probs = jnp.exp(scores - log_totals)
    grad_values = jnp.einsum(
        "rhqk,rqhd->rkhd",
        attn_probs.astype(jnp.bfloat16),
        grad_heads,
        preferred_element_type=jnp.float32,
    )
    grad_probs = jnp.einsum(
        "rqhd,rkhd->rhqk", grad_heads, value_heads, preferred_element_type=jnp.float32
    )
    grad_scores = attn_probs * (
        grad_probs - jnp.sum(grad_probs * attn_probs, axis=-1, keepdims=True)
    )
    grad_scores = grad_scores.astype(jnp.bfloat16)
    grad_queries = (
        jnp.einsum("rhqk,rkhd->rqhd", grad_scores, key_heads, preferred_element_type=jnp.float32)
        * scaling
    )
    grad_keys = (
        jnp.einsum("rhqk,rqhd->rkhd", grad_scores, query_heads, preferred_element_type=jnp.float32)
        * scaling
    )
    return (grad_queries.reshape(-1, D), grad_keys.reshape(-1, D), grad_values.reshape(-1, D))


def self_block(state, w_qkv, w_attn, allowed):
    state_low = state.astype(jnp.bfloat16)
    projected = product(state_low, w_qkv).astype(jnp.bfloat16)
    attended, log_totals = attend(
        projected[:, :D], projected[:, D : 2 * D], projected[:, 2 * D :], allowed
    )
    return (product(attended, w_attn), (state_low, projected, attended, log_totals))


def self_block_backward(stored, w_qkv, w_attn, allowed, grad_branch):
    state_low, projected, attended, log_totals = stored
    grad_low = grad_branch.astype(jnp.bfloat16)
    grad_w_attn = left_transposed(attended, grad_low)
    grad_attended = right_transposed(grad_low, w_attn).astype(jnp.bfloat16)
    grad_queries, grad_keys, grad_values = attend_backward(
        projected[:, :D],
        projected[:, D : 2 * D],
        projected[:, 2 * D :],
        allowed,
        log_totals,
        grad_attended,
    )
    grad_projected = jnp.concatenate([grad_queries, grad_keys, grad_values], axis=1).astype(
        jnp.bfloat16
    )
    grad_w_qkv = left_transposed(state_low, grad_projected)
    return (right_transposed(grad_projected, w_qkv), grad_w_qkv, grad_w_attn)


def feed_forward(hidden, w_in, b_in, w_out, b_out):
    hidden_low = hidden.astype(jnp.bfloat16)
    pre_gelu = product(hidden_low, w_in) + b_in
    activated = jax.nn.gelu(pre_gelu).astype(jnp.bfloat16)
    return (product(activated, w_out) + b_out, (hidden_low, pre_gelu, activated))


def feed_forward_backward(stored, w_in, w_out, grad_branch):
    hidden_low, pre_gelu, activated = stored
    grad_low = grad_branch.astype(jnp.bfloat16)
    grad_w_out = left_transposed(activated, grad_low)
    grad_b_out = jnp.sum(grad_low, axis=0, dtype=jnp.float32)
    grad_act = right_transposed(grad_low, w_out)
    grad_pre = jax.vjp(jax.nn.gelu, pre_gelu)[1](grad_act)[0].astype(jnp.bfloat16)
    grad_w_in = left_transposed(hidden_low, grad_pre)
    grad_b_in = jnp.sum(grad_pre, axis=0, dtype=jnp.float32)
    return (right_transposed(grad_pre, w_in), grad_w_in, grad_b_in, grad_w_out, grad_b_out)


def encoder_layer(state, params, allowed):
    w_qkv, w_attn, w_in, b_in, w_out, b_out, gain_rows, offsets = params
    branch, first_store = self_block(state, w_qkv, w_attn, allowed)
    hidden = layer_norm(state + branch, gain_rows[0], offsets[0])
    update, second_store = feed_forward(hidden, w_in, b_in, w_out, b_out)
    output = layer_norm(hidden + update, gain_rows[1], offsets[1])
    return (output, (branch, hidden, update, first_store, second_store))


def encoder_backward(state, params, allowed, grad_next):
    w_qkv, w_attn, w_in, b_in, w_out, b_out, gain_rows, offsets = params
    output, stored = encoder_layer(state, params, allowed)
    branch, hidden, update, first_store, second_store = stored
    grad_sum_two, grad_gain_two, grad_offset_two = norm_backward(
        hidden + update, gain_rows[1], offsets[1], grad_next
    )
    grad_hidden, grad_w_in, grad_b_in, grad_w_out, grad_b_out = feed_forward_backward(
        second_store, w_in, w_out, grad_sum_two
    )
    grad_sum_one, grad_gain_one, grad_offset_one = norm_backward(
        state + branch, gain_rows[0], offsets[0], grad_sum_two + grad_hidden
    )
    grad_state, grad_w_qkv, grad_w_attn = self_block_backward(
        first_store, w_qkv, w_attn, allowed, grad_sum_one
    )
    layer_grads = (
        grad_w_qkv,
        grad_w_attn,
        grad_w_in,
        grad_b_in,
        grad_w_out,
        grad_b_out,
        jnp.stack([grad_gain_one, grad_gain_two]),
        jnp.stack([grad_offset_one, grad_offset_two]),
    )
    return (grad_state + grad_sum_one, layer_grads)


def decoder_layer(
    state, memory_kv, params, cross_w, cross_gain_f, cross_bias_f, self_mask, cross_mask
):
    w_qkv, w_attn, w_in, b_in, w_out, b_out, gain_rows, offsets = params
    branch, first_store = self_block(state, w_qkv, w_attn, self_mask)
    hidden = layer_norm(state + branch, gain_rows[0], offsets[0])
    hidden_low = hidden.astype(jnp.bfloat16)
    cross_queries = product(hidden_low, cross_w[:, :D]).astype(jnp.bfloat16)
    cross_attended, cross_totals = attend(
        cross_queries, memory_kv[:, :D], memory_kv[:, D:], cross_mask
    )
    cross_branch = product(cross_attended, cross_w[:, D:])
    joined = layer_norm(hidden + cross_branch, cross_gain_f, cross_bias_f)
    update, second_store = feed_forward(joined, w_in, b_in, w_out, b_out)
    output = layer_norm(joined + update, gain_rows[1], offsets[1])
    return (
        output,
        (
            branch,
            hidden,
            hidden_low,
            cross_queries,
            cross_attended,
            cross_totals,
            cross_branch,
            joined,
            update,
            first_store,
            second_store,
        ),
    )


def decoder_backward(
    state, memory_kv, params, cross_w, cross_gain_f, cross_bias_f, self_mask, cross_mask, grad_next
):
    w_qkv, w_attn, w_in, b_in, w_out, b_out, gain_rows, offsets = params
    output, stored = decoder_layer(
        state, memory_kv, params, cross_w, cross_gain_f, cross_bias_f, self_mask, cross_mask
    )
    (
        branch,
        hidden,
        hidden_low,
        cross_queries,
        cross_attended,
        cross_totals,
        cross_branch,
        joined,
        update,
        first_store,
        second_store,
    ) = stored
    grad_sum_three, grad_gain_two, grad_offset_two = norm_backward(
        joined + update, gain_rows[1], offsets[1], grad_next
    )
    grad_joined, grad_w_in, grad_b_in, grad_w_out, grad_b_out = feed_forward_backward(
        second_store, w_in, w_out, grad_sum_three
    )
    grad_sum_two, grad_cross_gain, grad_cross_bias = norm_backward(
        hidden + cross_branch, cross_gain_f, cross_bias_f, grad_sum_three + grad_joined
    )
    grad_cross_low = grad_sum_two.astype(jnp.bfloat16)
    grad_cross_out = left_transposed(cross_attended, grad_cross_low)
    grad_cross_attended = right_transposed(grad_cross_low, cross_w[:, D:]).astype(jnp.bfloat16)
    grad_queries, grad_keys, grad_values = attend_backward(
        cross_queries,
        memory_kv[:, :D],
        memory_kv[:, D:],
        cross_mask,
        cross_totals,
        grad_cross_attended,
    )
    grad_queries = grad_queries.astype(jnp.bfloat16)
    grad_cross_query = left_transposed(hidden_low, grad_queries)
    grad_hidden = grad_sum_two + right_transposed(grad_queries, cross_w[:, :D])
    grad_sum_one, grad_gain_one, grad_offset_one = norm_backward(
        state + branch, gain_rows[0], offsets[0], grad_hidden
    )
    grad_state, grad_w_qkv, grad_w_attn = self_block_backward(
        first_store, w_qkv, w_attn, self_mask, grad_sum_one
    )
    layer_grads = (
        grad_w_qkv,
        grad_w_attn,
        grad_w_in,
        grad_b_in,
        grad_w_out,
        grad_b_out,
        jnp.stack([grad_gain_one, grad_gain_two]),
        jnp.stack([grad_offset_one, grad_offset_two]),
        jnp.concatenate([grad_cross_query, grad_cross_out], axis=1),
        grad_cross_gain,
        grad_cross_bias,
    )
    return (
        output,
        grad_state + grad_sum_one,
        layer_grads,
        jnp.concatenate([grad_keys, grad_values], axis=1),
    )


def body(
    token_rows,
    lengths,
    self_qkv,
    self_out,
    ffn_in,
    ffn_in_bias,
    ffn_out,
    ffn_out_bias,
    norm_gain,
    norm_bias,
    cross_weights,
    cross_gain,
    cross_bias,
    output_grad,
):
    is_encoder = lax.axis_index("section") == 0
    row_len = token_rows.shape[1] // lengths.shape[0]
    source_ids = segment_ids(lengths[:, 0], row_len)
    target_ids = segment_ids(lengths[:, 1], row_len)
    places = jnp.arange(row_len, dtype=jnp.int32)
    enc_mask = source_ids[:, :, None] == source_ids[:, None, :]
    dec_mask = (target_ids[:, :, None] == target_ids[:, None, :]) & (
        places[:, None] >= places[None, :]
    )[None]
    cross_mask = target_ids[:, :, None] == source_ids[:, None, :]
    rows_in = token_rows[0].astype(jnp.float32)
    tokens = rows_in.shape[0]
    params = (
        self_qkv[0],
        self_out[0],
        ffn_in[0],
        ffn_in_bias[0].astype(jnp.float32),
        ffn_out[0],
        ffn_out_bias[0].astype(jnp.float32),
        norm_gain[0].astype(jnp.float32),
        norm_bias[0].astype(jnp.float32),
    )
    cross_w = cross_weights[0]
    cross_gain_f = cross_gain.astype(jnp.float32)
    cross_bias_f = cross_bias.astype(jnp.float32)
    zero_rows = jnp.zeros_like(rows_in)
    zero_kv = jnp.zeros((tokens, 2 * D), jnp.bfloat16)
    zero_grads = tuple((jnp.zeros(weight.shape, jnp.float32) for weight in params))
    zero_cross = jnp.zeros(cross_w.shape, jnp.float32)
    zero_norm = jnp.zeros(cross_gain.shape, jnp.float32)
    zero_full = zero_grads + (zero_cross, zero_norm, zero_norm)

    def encode():
        states = [rows_in]
        for repeat in range(REPEATS):
            states.append(encoder_layer(states[-1], params, enc_mask)[0])
        memory_kv = product(states[-1].astype(jnp.bfloat16), cross_w).astype(jnp.bfloat16)
        return (jnp.stack(states[1:]), memory_kv)

    def encode_blank():
        return (jnp.zeros((REPEATS, tokens, D), jnp.float32), zero_kv)

    recurrent, memory_kv = lax.cond(is_encoder, encode, encode_blank)
    kv_in = from_behind(memory_kv, "section", 1)

    def decode():
        states = [rows_in]
        repeat = 0
        states.append(
            decoder_layer(
                states[-1], kv_in, params, cross_w, cross_gain_f, cross_bias_f, dec_mask, cross_mask
            )[0]
        )
        grad_next = output_grad.astype(jnp.float32)
        grad_kv = jnp.zeros((tokens, 2 * D), jnp.float32)
        last_set = zero_full
        rest_set = zero_full
        decoded = zero_rows
        for repeat in reversed(range(REPEATS)):
            output, grad_next, layer_grads, grad_memory = decoder_backward(
                states[repeat],
                kv_in,
                params,
                cross_w,
                cross_gain_f,
                cross_bias_f,
                dec_mask,
                cross_mask,
                grad_next,
            )
            if repeat == REPEATS - 1:
                decoded = output
                last_set = layer_grads
            else:
                rest_set = jax.tree.map(jnp.add, rest_set, layer_grads)
            grad_kv = grad_kv + grad_memory
        return (decoded, grad_next, last_set, rest_set, grad_kv.astype(jnp.bfloat16))

    def decode_blank():
        return (zero_rows, zero_rows, zero_full, zero_full, zero_kv)

    decoded, dec_rows_grad, dec_last, dec_rest, kv_grad = lax.cond(
        jnp.logical_not(is_encoder), decode, decode_blank
    )
    kv_back = from_behind(kv_grad, "section", -1)
    gain_sum, offset_sum = lax.psum(
        (dec_last[9] + dec_rest[9], dec_last[10] + dec_rest[10]), ("section", "dp")
    )

    def encode_back_last():
        memory_low = recurrent[REPEATS - 1].astype(jnp.bfloat16)
        grad_cross = left_transposed(memory_low, kv_back)
        grad_next = right_transposed(kv_back, cross_w)
        layer_input = recurrent[REPEATS - 2]
        grad_next, layer_grads = encoder_backward(layer_input, params, enc_mask, grad_next)
        return (grad_next, layer_grads, grad_cross)

    def encode_back_last_blank():
        return (zero_rows, zero_grads, zero_cross)

    enc_next, enc_last, enc_cross = lax.cond(is_encoder, encode_back_last, encode_back_last_blank)
    enc_last_set = enc_last + (enc_cross,)

    def encode_back_rest():
        grad_next = enc_next
        summed = zero_grads
        for repeat in reversed(range(REPEATS - 1)):
            grad_next, layer_grads = encoder_backward(rows_in, params, enc_mask, grad_next)
            summed = jax.tree.map(jnp.add, summed, layer_grads)
        return (grad_next, summed)

    def encode_back_rest_blank():
        return (enc_next, zero_grads)

    enc_rows_grad, enc_rest = lax.cond(is_encoder, encode_back_rest, encode_back_rest_blank)
    enc_rest_set = enc_rest + (zero_cross,)
    enc_all = jax.tree.map(jnp.add, enc_last_set, enc_rest_set)
    dec_all = jax.tree.map(jnp.add, dec_last[:9], dec_rest[:9])
    joined = jax.tree.map(jnp.add, enc_all, dec_all)
    totals = lax.psum(
        (
            joined[0],
            joined[1],
            joined[2],
            joined[3],
            joined[4],
            joined[5],
            joined[6],
            joined[7],
            joined[8],
        ),
        "dp",
    )
    layer_out = (recurrent[REPEATS - 1] + decoded).astype(jnp.bfloat16)
    rows_grad = jnp.where(is_encoder, enc_rows_grad, dec_rows_grad)
    return (
        layer_out[None],
        rows_grad[None],
        totals[0][None],
        totals[1][None],
        totals[2][None],
        totals[3][None],
        totals[4][None],
        totals[5][None],
        totals[6][None],
        totals[7][None],
        totals[8][None],
        gain_sum,
        offset_sum,
    )


def solution(mesh):
    in_specs = (
        P("section", "dp", None),
        P("dp", None, None),
        P("section", None, None),
        P("section", None, None),
        P("section", None, None),
        P("section", None),
        P("section", None, None),
        P("section", None),
        P("section", None, None),
        P("section", None, None),
        P("section", None, None),
        P(),
        P(),
        P("dp", None),
    )
    out_specs = (
        P("section", "dp", None),
        P("section", "dp", None),
        P("section", None, None),
        P("section", None, None),
        P("section", None, None),
        P("section", None),
        P("section", None, None),
        P("section", None),
        P("section", None, None),
        P("section", None, None),
        P("section", None, None),
        P(),
        P(),
    )
    return jax.shard_map(body, mesh=mesh, in_specs=in_specs, out_specs=out_specs, check_vma=False)
```

profile of v0, /device:TPU:0, one launch (start us, length us, event | category | flops | bytes accessed | tf_op | source)
XLA Modules:
  0.0 779.1 jit_solution(11977542986278891606)
XLA Ops:
  12.9 61.7 %conditional.4 = (f32[2,512,512]{1,2,0:T(8,128)}, bf16[512,1024]{1,0:T(8,128)(2,1)}, f32[512,512]{1,0:T(8,128)}) conditional(s32[]{:T(128)} %convert_element_type.529, () %tuple.45, (f32[512,512]{0,1:T(8,128)S(1)}, bf16[512,1536]{1,0:T(8,128)(2,1)}, pred[1,512,512]{1,2,0:T(8,128)(4,1)}, bf16[512,512]{1,0:T(8,128)(2,1)}, f32[2,512]{1,0:T(2,128)S(1)}, ...), branch_computations={%region_2.3_spmd, %region_3.16_spmd} | conditional | flops 8117816320 | bytes 138092864 | solution.py:369
  13.9 2.4 convolution_convert_fusion.1
  17.1 6.2 fusion.278
  23.4 4.4 fusion.31
  29.5 6.5 fusion.280
  37.4 2.9 convolution_convert_fusion
  46.5 7.7 fusion.283
  54.2 4.3 fusion.30
  60.0 6.9 fusion.285
  74.7 2.4 copy.244
  77.2 2.3 collective-permute-start
  79.7 22.4 %collective-permute-done = bf16[512,1024]{0,1:T(8,128)(2,1)} collective-permute-done((bf16[512,1024]{0,1:T(8,128)(2,1)}, bf16[512,1024]{0,1:T(8,128)(2,1)}, u32[]{:S(2)}, u32[]{:S(2)}) %collective-permute-start) | collective-permute-done | bytes 1048608 | tf_op jit(solution)/shard_map/ppermute | solution.py:19
  105.4 37.9 %conditional.5 = (f32[512,512]{0,1:T(8,128)}, f32[512,1536]{1,0:T(8,128)}, f32[512,512]{1,0:T(8,128)}, f32[512,2048]{1,0:T(8,128)}, f32[2048]{0:T(1024)}, /*inde...) conditional(s32[]{:T(128)} %convert_element_type.541, () %tuple.47, ...), branch_computations={%region_17.18_spmd.clone, %region_18.72_spmd.clone} | conditional | flops 29320781824 | bytes 980472896 | solution.py:408
  123.8 2.5 broadcast_in_dim.388.clone
  126.3 2.4 broadcast_in_dim.386.clone
  128.8 2.5 broadcast_in_dim.388
  131.3 2.5 broadcast_in_dim.386
  146.8 185.1 %collective-permute-done.1 = bf16[512,1024]{1,0:T(8,128)(2,1)} collective-permute-done((bf16[512,1024]{1,0:T(8,128)(2,1)}, bf16[512,1024]{1,0:T(8,128)(2,1)}, u32[]{:S(2)}, u32[]{:S(2)}) %collective-permute-start.1) | collective-permute-done | bytes 1048608 | tf_op jit(solution)/shard_map/ppermute | solution.py:19
  331.9 63.2 %conditional.6 = (f32[512,512]{1,0:T(8,128)}, f32[512,512]{1,0:T(8,128)}, f32[512,2048]{1,0:T(8,128)}, f32[2048]{0:T(1024)S(1)}, f32[2048,512]{1,0:T(8,128)}, /*...) conditional(s32[]{:T(128)} %convert_element_type.529, () %tuple.49, ...), branch_computations={%region_72.73_spmd, %region_73.91_spmd} | conditional | flops 12458389504 | bytes 222968048 | solution.py:427
  333.4 2.9 copy.249
  336.3 2.7 convolution_convert_fusion.3
  345.5 3.6 fusion.102
  349.2 2.5 fusion.290
  361.8 4.1 convert_reduce_fusion
  365.9 4.1 fusion.115
  375.8 3.4 fusion.111
  381.3 3.0 multiply_convert_fusion
  388.5 2.8 convolution_bitcast_fusion
  391.3 3.6 copy.306
  395.1 4.1 add_bitcast_fusion.3
  399.2 56.9 %conditional.7 = (f32[512,512]{0,1:T(8,128)S(1)}, f32[512,512]{1,0:T(8,128)}, f32[512,2048]{1,0:T(8,128)}, f32[2048]{0:T(1024)S(1)}, f32[2048,512]{1,0:T(8,128)}...) conditional(s32[]{:T(128)} %convert_element_type.529, ...), branch_computations={%region_91.92_spmd, %region_92.110_spmd} | conditional | flops 11385171968 | bytes 213006560 | solution.py:441
  401.2 2.5 copy.251
  404.5 2.7 convolution_convert_fusion.5
  413.8 2.6 fusion.295
  424.7 4.1 convert_reduce_fusion.2
  428.8 4.1 fusion.148
  438.2 3.3 fusion.144
  443.7 2.6 multiply_convert_fusion.4
  449.5 2.8 convolution_bitcast_fusion.1
  452.3 3.5 copy.308
  456.1 10.3 %add_bitcast_fusion = f32[1,2048,512]{2,1,0:T(8,128)} fusion(f32[2048,512]{1,0:T(8,128)} %get-tuple-element.292, f32[2048,512]{1,0:T(8,128)} %get-tuple-element.293, f32[2048,512]{1,0:T(8,128)} %get-tuple-element.290, f32[2048,512]{1,0:T(8,128)} %get-tuple-element.291), kind=kLoop, calls=%fused_computation.472 | loop fusion | flops 3145728 | bytes 20971520 | tf_op jit(solution)/shard_map/broadcast_in_dim | solution.py:469
  466.4 10.2 %add_bitcast_fusion.1 = f32[1,512,2048]{2,1,0:T(8,128)} fusion(f32[512,2048]{1,0:T(8,128)} %get-tuple-element.284, f32[512,2048]{1,0:T(8,128)} %get-tuple-element.285, f32[512,2048]{1,0:T(8,128)} %get-tuple-element.282, f32[512,2048]{1,0:T(8,128)} %get-tuple-element.283), kind=kLoop, calls=%fused_computation.473 | loop fusion | flops 3145728 | bytes 20971520 | tf_op jit(solution)/shard_map/broadcast_in_dim | solution.py:467
  476.6 3.6 add_bitcast_fusion.4
  480.2 7.7 add_bitcast_fusion.2
  491.0 41.5 %all-reduce = (f32[512]{0:T(512)}, f32[512]{0:T(512)}) all-reduce(f32[512]{0:T(512)S(1)} %add.707, f32[512]{0:T(512)S(1)} %add.708), channel_id=1, replica_groups=mesh['section'=2,'dp'=16] {'section','dp'}, use_global_device_ids=true, to_apply=%region_119.120 | all-reduce | flops 1024 | bytes 8192 | tf_op jit(solution)/shard_map/psum | solution.py:412
  538.0 63.4 %all-reduce.1 = (f32[1,2048]{1,0:T(1,128)}, f32[1,512]{1,0:T(1,128)}, f32[1,2,512]{2,1,0:T(2,128)}, f32[1,2,512]{2,1,0:T(2,128)}) all-reduce(f32[1,2048]{1,0:T(1,128)S(1)} %bitcast.611, f32[1,512]{1,0:T(1,128)S(1)} %bitcast.638, f32[1,2,512]{2,1,0:T(2,128)S(1)} %add_bitcast_fusion.6, ...), channel_id=1, replica_groups=mesh['section'=2,'dp'=16] {'dp'}, use_global_device_ids=true, to_apply=%region_113.114 | all-reduce | flops 4608 | bytes 36864 | tf_op jit(solution)/shard_map/psum | solution.py:446
  602.6 156.2 %all-reduce.5.cloned.1.call-done = (f32[1,512,1536]{2,1,0:T(8,128)}, f32[1,512,512]{2,1,0:T(8,128)}, f32[1,512,2048]{2,1,0:T(8,128)}, f32[1,2048,512]{2,1,0:T(8,128)}, f32[1,512,1024]{2,1,0:T(8,128)}) async-done(((f32[1,512,1536]{2,1,0:T(8,128)}, f32[1,512,512]{2,1,0:T(8,128)}, f32[1,512,2048]{2,1,0:T(8,128)}, f32[1,2048,512]{2,1,0:T(8,128)}, f32[1,512,1024]{2,1,0:T(8,128)}), (f32[1,512,1536]{2,1,0:T(8,128)}, ...) | async-done | bytes 14680080 | tf_op jit(solution)/shard_map/psum | solution.py:446
  758.8 3.9 copy.423
  (224 shorter events, 128.3 us)
Async XLA Ops:
  7.2 751.7 %all-reduce.5.cloned.1.call-start = ((), (), s32[]{:S(2)}) async-start(), calls=%async_computation | async-start | bytes 29360128 | tf_op jit(solution)/shard_map/psum | solution.py:446
  12.0 1.0 copy-start.9
  12.7 92.6 %copy-start.73 = (f32[2,512]{1,0:T(2,128)}, f32[2,512]{1,0:T(2,128)S(1)}, u32[]{:S(2)}) copy-start(f32[2,512]{1,0:T(2,128)S(1)} %get-tuple-element.777) | copy-start | bytes 12292
  12.7 92.6 %copy-start.74 = (f32[2,512]{1,0:T(2,128)}, f32[2,512]{1,0:T(2,128)S(1)}, u32[]{:S(2)}) copy-start(f32[2,512]{1,0:T(2,128)S(1)} %get-tuple-element.776) | copy-start | bytes 12292
  12.7 66.9 %copy-start.81 = (bf16[512]{0:T(512)(128)(2,1)S(1)}, bf16[512]{0:T(512)(128)(2,1)}, u32[]{:S(2)}) copy-start(bf16[512]{0:T(512)(128)(2,1)} %param.33) | copy-start | bytes 3076
  12.7 66.9 %copy-start.82 = (bf16[512]{0:T(512)(128)(2,1)S(1)}, bf16[512]{0:T(512)(128)(2,1)}, u32[]{:S(2)}) copy-start(bf16[512]{0:T(512)(128)(2,1)} %param.34) | copy-start | bytes 3076
  12.9 1.0 copy-start.10
  23.4 4.4 copy-start.4
  23.4 4.4 copy-start.11
  27.7 1.8 copy-start.6
  28.3 1.0 copy-start.51
  46.5 7.7 copy-start.68
  54.2 4.3 copy-start.21
  59.1 1.0 copy-start.50
  60.0 8.2 %copy-start.22 = (f32[512,512]{0,1:T(8,128)S(1)}, f32[512,512]{0,1:T(8,128)}, u32[]{:S(2)}) copy-start(f32[512,512]{0,1:T(8,128)} %get-tuple-element.680) | copy-start | bytes 3145732 | tf_op jit(solution)/shard_map/cond
  69.9 2.9 copy-start.16
  74.7 30.7 %copy-start.3 = (bf16[1,512,512]{2,1,0:T(8,128)(2,1)S(1)}, bf16[1,512,512]{2,1,0:T(8,128)(2,1)}, u32[]{:S(2)}) copy-start(bf16[1,512,512]{2,1,0:T(8,128)(2,1)} %param.25) | copy-start | bytes 1572868
  74.7 30.7 %copy-start.5 = (bf16[1,512,2048]{2,1,0:T(8,128)(2,1)S(1)}, bf16[1,512,2048]{2,1,0:T(8,128)(2,1)}, u32[]{:S(2)}) copy-start(bf16[1,512,2048]{2,1,0:T(8,128)(2,1)} %param.26) | copy-start | bytes 6291460
  74.7 30.7 %copy-start.67 = (bf16[512,512]{1,0:T(8,128)(2,1)S(1)}, bf16[512,512]{1,0:T(8,128)(2,1)}, u32[]{:S(2)}) copy-start(bf16[512,512]{1,0:T(8,128)(2,1)} %param.35) | copy-start | bytes 1572868
  77.2 24.9 %collective-permute-start = (bf16[512,1024]{0,1:T(8,128)(2,1)}, bf16[512,1024]{0,1:T(8,128)(2,1)}, u32[]{:S(2)}, u32[]{:S(2)}) collective-permute-start(bf16[512,1024]{0,1:T(8,128)(2,1)} %copy.244), channel_id=1, source_target_pairs={{0,16},{1,17},{2,18},{3,19},{4,20},{5,21},{6,22},{7,23},{8,24},{9,... | collective-permute-start | bytes 3145736 | tf_op jit(solution)/shard_map/ppermute | solution.py:19
  145.5 186.4 %collective-permute-start.1 = (bf16[512,1024]{1,0:T(8,128)(2,1)}, bf16[512,1024]{1,0:T(8,128)(2,1)}, u32[]{:S(2)}, u32[]{:S(2)}) collective-permute-start(bf16[512,1024]{1,0:T(8,128)(2,1)} %copy.248), channel_id=1, source_target_pairs={{16,0},{17,1},{18,2},{19,3},{20,4},{21,5},{22,6},{23,7},{24,8},{25... | collective-permute-start | bytes 3145736 | tf_op jit(solution)/shard_map/ppermute | solution.py:19
  345.5 3.6 copy-start.35
  351.7 1.2 copy-start.56
  352.9 1.6 copy-start.30
  355.0 1.6 copy-start.86
  356.7 2.2 copy-start.20
  384.3 2.2 copy-start.91
  416.4 1.2 copy-start.57
  417.6 1.6 copy-start.13
  419.7 1.6 copy-start.87
  421.4 2.4 copy-start.23
  443.7 2.6 copy-start.36
  446.3 2.2 copy-start.92
  456.1 10.4 %copy-start.46 = (f32[512,512]{0,1:T(8,128)}, f32[512,512]{0,1:T(8,128)S(1)}, u32[]{:S(2)}) copy-start(f32[512,512]{0,1:T(8,128)S(1)} %get-tuple-element.272) | copy-start | bytes 3145732
  488.0 46.8 %copy-start.47 = (f32[512,512]{0,1:T(8,128)S(1)}, f32[512,512]{0,1:T(8,128)}, u32[]{:S(2)}) copy-start(f32[512,512]{0,1:T(8,128)} %copy-done.46) | copy-start | bytes 3145732
  758.8 3.9 copy-start.64
  758.8 4.9 copy-start.44
  763.7 3.7 copy-start.43
  767.4 3.1 copy-start.58
Sparse Core Ops, SparseCore 0:
  488.1 270.6 all-reduce.4
where the time goes:
time: 784 us; the launch traced here: 779 us
  waiting for transfers between devices  364 us (46%)
  matrix products  122 us (16%)
  blocking collectives  105 us (13%)
  local copies, waits for them, and re-layouts  93.3 us (12%)
  other arithmetic  66.1 us (8%)
  between operations  14.7 us (2%)
  loops' own time  10.7 us (1%)
    ppermute x2, waiting for transfers between devices, from_behind(): return lax.ppermute(shard, axis, pairs)  207 us
    psum x1, waiting for transfers between devices, body(): lax.psum((joined[0], joined[1], joined[2], joined[3], joined[4], joined[5...  156 us
    psum x1, blocking collectives, body(): lax.psum((joined[0], joined[1], joined[2], joined[3], joined[4], joined[5...  63.4 us
    psum x1, blocking collectives, body(): lax.psum((dec_last[9] + dec_rest[9], dec_last[10] + dec_rest[10]), ('sect...  41.5 us
    dot_general x15, matrix products, product(): return jnp.dot(former, latter, preferred_element_type=jnp.float32)  34.9 us
    dot_general x9, matrix products, left_transposed(): lax.dot_general(former, latter, (((0,), (0,)), ((), ())), preferred_eleme...  27.1 us
    dot_general x9, matrix products, right_transposed(): lax.dot_general(former, latter, (((1,), (1,)), ((), ())), preferred_eleme...  17.8 us
    another operation x16, local copies, waits for them, and re-layouts  15.8 us
  transfers between devices with their start and end apart: 3, of which 3 were waited for; matrix products, arithmetic and copies ran while one was open for 1% of the time, Pallas kernels for 0%

commit v1 on v0

v1 whole, which is shorter than its diff:
```python
import types

import jax
import jax.numpy as jnp
from jax import lax
from jax.experimental import pallas as pl
from jax.experimental.pallas import tpu as pltpu
from jax.sharding import PartitionSpec as P

BF, F32 = jnp.bfloat16, jnp.float32
D, FF, HEAD_DIM, SENTS, REPEATS = 512, 2048, 64, 8, 2
T = 512
WIN = 128
EPSILON = 1e-05
MASKED = -1e9
SCALE = HEAD_DIM**-0.5
LOG2E = 1.4426950408889634
K0 = 0.7978845608028654
K1 = K0 * 0.044715
UNROLL = 4
VMEM_LIMIT = 60 * 2**20


def nn(a, b):
    return lax.dot_general(a, b, (((1,), (0,)), ((), ())), preferred_element_type=F32)


def nt(a, b):
    return lax.dot_general(a, b, (((1,), (1,)), ((), ())), preferred_element_type=F32)


def tn(a, b):
    return lax.dot_general(a, b, (((0,), (0,)), ((), ())), preferred_element_type=F32)


def iota(axis):
    return lax.broadcasted_iota(jnp.int32, (WIN, WIN), axis)


def halves():
    lane = lax.broadcasted_iota(jnp.int32, (1, WIN), 1)
    even = jnp.where(lane < HEAD_DIM, 1.0, 0.0).astype(BF)
    odd = jnp.where(lane < HEAD_DIM, 0.0, 1.0).astype(BF)
    return even, odd


def wide(ref, rows):
    part = ref[rows, :]
    return jnp.concatenate([part] * (D // WIN), 1)


def chunks(size=256):
    return [slice(i, i + size) for i in range(0, T, size)]


def prepare(lens, starts):
    for side in range(2):
        total = jnp.int32(0)
        for j in range(SENTS):
            starts[side, j] = total
            total = total + lens[0, side, j]


def window(lens, starts, side, s):
    first = starts[side, s]
    base = pl.multiple_of(jnp.minimum((first // 16) * 16, T - WIN), 16)
    return base, first - base, first - base + lens[0, side, s]


def sentences(body):
    @pl.loop(0, SENTS // UNROLL)
    def _(j):
        for t in range(UNROLL):
            body(j * UNROLL + t)


def attend(q, qc, k, kc, v, vc, out, probs, lens, starts, qside, kside, lim):
    even, odd = halves()
    row, col = iota(0), iota(1)

    def body(s):
        wq, lo, hi = window(lens, starts, qside, s)
        wk, klo, khi = (wq, lo, hi) if kside is qside else window(lens, starts, kside, s)
        valid = (row >= klo) & (row < khi)
        if lim is not None:
            valid = valid & (row - col <= lim)
        mine = (row >= lo) & (row < hi)
        for g in range(4):
            qs = q[pl.ds(wq, WIN), qc + g * WIN : qc + (g + 1) * WIN]
            ks = k[pl.ds(wk, WIN), kc + g * WIN : kc + (g + 1) * WIN]
            vs = v[pl.ds(wk, WIN), vc + g * WIN : vc + (g + 1) * WIN]
            scores = nt(ks, jnp.concatenate([qs * even, qs * odd], 0))
            parts = []
            for h in range(2):
                x = jnp.where(valid, scores[:, h * WIN : (h + 1) * WIN] * (SCALE * LOG2E), MASKED)
                p = jnp.exp2(x - jnp.max(x, 0, keepdims=True))
                parts.append((p * (1.0 / jnp.sum(p, 0, keepdims=True))).astype(BF))
            probs[s, :, g * 2 * WIN : (g + 1) * 2 * WIN] = jnp.concatenate(parts, 1)
            turned = jnp.concatenate([parts[0].T, parts[1].T], 1)
            r = nn(turned, jnp.concatenate([vs * even, vs * odd], 0))
            place = (pl.ds(wq, WIN), slice(g * WIN, (g + 1) * WIN))
            out[place] = jnp.where(mine, r, out[place].astype(F32)).astype(BF)

    sentences(body)


def attend_backward(q, qc, k, kc, v, vc, probs, grad, dq, dkv, lens, starts, qside, kside):
    even, odd = halves()
    row = iota(0)

    def body(s):
        wq, lo, hi = window(lens, starts, qside, s)
        wk, klo, khi = (wq, lo, hi) if kside is qside else window(lens, starts, kside, s)
        mine = (row >= lo) & (row < hi)
        theirs = (row >= klo) & (row < khi)
        keep = jnp.where(mine, 1.0, 0.0).astype(BF)
        keep_even, keep_odd = keep * even, keep * odd
        for g in range(4):
            qs = q[pl.ds(wq, WIN), qc + g * WIN : qc + (g + 1) * WIN]
            ks = k[pl.ds(wk, WIN), kc + g * WIN : kc + (g + 1) * WIN]
            vs = v[pl.ds(wk, WIN), vc + g * WIN : vc + (g + 1) * WIN]
            go = grad[pl.ds(wq, WIN), g * WIN : (g + 1) * WIN]
            both_g = jnp.concatenate([go * keep_even, go * keep_odd], 0)
            both_q = jnp.concatenate([qs * even, qs * odd], 0)
            p_low = probs[s, :, g * 2 * WIN : (g + 1) * 2 * WIN]
            p = p_low.astype(F32)
            dp = nt(vs, both_g)
            ds = (p * (dp - jnp.sum(p * dp, 0, keepdims=True))).astype(BF)
            dv = nn(p_low, both_g)
            dk = nn(ds, both_q) * SCALE
            turned = jnp.concatenate([ds[:, :WIN].T, ds[:, WIN:].T], 1)
            dqs = nn(turned, jnp.concatenate([ks * even, ks * odd], 0)) * SCALE
            ref, c = dq
            place = (pl.ds(wq, WIN), slice(c + g * WIN, c + (g + 1) * WIN))
            ref[place] = jnp.where(mine, dqs, ref[place].astype(F32)).astype(BF)
            ref, c_k, c_v, adds = dkv
            for c, value in ((c_k, dk), (c_v, dv)):
                place = (pl.ds(wk, WIN), slice(c + g * WIN, c + (g + 1) * WIN))
                if adds:
                    ref[place] += value
                else:
                    ref[place] = jnp.where(theirs, value, ref[place].astype(F32)).astype(BF)

    sentences(body)


def normed(v):
    centre = v - jnp.mean(v, -1, keepdims=True)
    rstd = lax.rsqrt(jnp.mean(centre * centre, -1, keepdims=True) + EPSILON)
    return centre * rstd, rstd


def norm_out(v, rows, xh, rs, gain, bias, wide_ref, low_ref):
    xhat, rstd = normed(v)
    xh[rows, :] = xhat.astype(BF)
    rs[rows, :] = jnp.broadcast_to(rstd, (v.shape[0], WIN))
    h = xhat * gain + bias
    wide_ref[rows, :] = h
    low_ref[rows, :] = h.astype(BF)


def norm_backward(dst, xh, rs, gain, low, vec, gain_row, bias_row):
    for rows in chunks():
        dy = dst[rows, :]
        xhat = xh[rows, :].astype(F32)
        rstd = wide(rs, rows)
        prod = dy * xhat
        vec[gain_row : gain_row + 1, :] += jnp.sum(prod, 0, keepdims=True)
        vec[bias_row : bias_row + 1, :] += jnp.sum(dy, 0, keepdims=True)
        scaled = dy * gain
        m1 = jnp.mean(scaled, -1, keepdims=True)
        m2 = jnp.mean(prod * gain, -1, keepdims=True)
        ds = rstd * (scaled - m1 - xhat * m2)
        dst[rows, :] = ds
        low[rows, :] = ds.astype(BF)


def self_forward(x, low, w_qkv, w_out, qkv, att, probs, xh, rs, gain, bias, h, h_low, lens, starts, side, lim):
    for c in range(3):
        cols = slice(c * D, (c + 1) * D)
        qkv[:, cols] = nn(low[...], w_qkv[:, cols]).astype(BF)
    attend(qkv, 0, qkv, D, qkv, 2 * D, att, probs, lens, starts, side, side, lim)
    for rows in chunks():
        norm_out(x[rows, :] + nn(att[rows, :], w_out[...]), rows, xh, rs, gain, bias, h, h_low)


def self_tail(dst, da, w_out, tmp, qkv, probs, dqkv, w_qkv, lens, starts, side):
    tmp[...] = nt(da[...], w_out[...]).astype(BF)
    attend_backward(
        qkv, 0, qkv, D, qkv, 2 * D, probs, tmp, (dqkv, 0), (dqkv, D, 2 * D, False), lens, starts, side, side
    )
    for rows in chunks():
        dst[rows, :] += nt(dqkv[rows, :], w_qkv[...])


def self_backward(dst, xh, rs, gain, vec, da, w_out, tmp, qkv, probs, dqkv, w_qkv, lens, starts, side):
    norm_backward(dst, xh, rs, gain, da, vec, 5, 7)
    self_tail(dst, da, w_out, tmp, qkv, probs, dqkv, w_qkv, lens, starts, side)


def ffn_forward(h, h_low, w_in, b_in, w_out, b_out, z, gd, xh, rs, gain, bias, out, out_low):
    for c in range(4):
        cols = slice(c * D, (c + 1) * D)
        u = nn(h_low[...], w_in[:, cols]) + b_in[:, cols].astype(F32)
        square = u * u
        half = 0.5 + 0.5 * jnp.tanh(u * (K0 + K1 * square))
        act = u * half
        z[:, cols] = act.astype(BF)
        gd[:, cols] = (half + act * (1.0 - half) * (2.0 * K0 + 6.0 * K1 * square)).astype(BF)
    for rows in chunks():
        v = h[rows, :] + (nn(z[rows, :], w_out[...]) + b_out[...].astype(F32))
        norm_out(v, rows, xh, rs, gain, bias, out, out_low)


def ffn_backward(dst, xh, rs, gain, vec, dz, gdu, w_in, w_out):
    norm_backward(dst, xh, rs, gain, dz, vec, 6, 8)
    vec[4:5, :] += jnp.sum(dz[...].astype(F32), 0, keepdims=True)
    for c in range(4):
        cols = slice(c * D, (c + 1) * D)
        du = (nt(dz[...], w_out[cols, :]) * gdu[:, cols].astype(F32)).astype(BF)
        gdu[:, cols] = du
        vec[c : c + 1, :] += jnp.sum(du.astype(F32), 0, keepdims=True)
    for rows in chunks():
        dst[rows, :] += nt(gdu[rows, :], w_in[...])


def rows_of(ref):
    return ref[...].reshape(2 * T, ref.shape[-1])


class Copies:
    def __init__(self, sems):
        self.sems, self.used = sems, 0

    def slots(self, count=1):
        first = self.used
        self.used += count
        return first

    def make(self, src, dst, slot=None):
        slot = self.slots() if slot is None else slot
        return pltpu.make_async_copy(src, dst, self.sems.at[slot])

    def table(self, **pairs):
        return types.SimpleNamespace(**{n: self.make(a, b) for n, (a, b) in pairs.items()})


def every(table):
    return list(vars(table).values())


HERE, VMEM, SMEM = pl.ANY, pltpu.VMEM, pltpu.SMEM


def phase(body, ins, outs, scratch, flops, n_sems=64):
    in_names, out_names, names = list(ins), list(outs), list(scratch)

    def kernel(*refs):
        labels = in_names + out_names + ["v_" + n for n in names]
        r = types.SimpleNamespace(**dict(zip(labels, refs)))
        r.starts, r.sems = refs[-2:]
        body(r)

    moved = sum(a.size * a.dtype.itemsize for a, _ in ins.values())
    results = pl.pallas_call(
        kernel,
        name=body.__name__,
        in_specs=[pl.BlockSpec(memory_space=s) for _, s in ins.values()],
        out_specs=[pl.BlockSpec(memory_space=HERE)] * len(outs),
        out_shape=[jax.ShapeDtypeStruct(s, d) for s, d in outs.values()],
        scratch_shapes=[VMEM(s, d) for s, d in scratch.values()]
        + [SMEM((2, SENTS), jnp.int32), pltpu.SemaphoreType.DMA((n_sems,))],
        compiler_params=pltpu.CompilerParams(vmem_limit_bytes=VMEM_LIMIT),
        cost_estimate=pl.CostEstimate(flops=flops, bytes_accessed=moved, transcendentals=0),
    )(*[a for a, _ in ins.values()])
    return types.SimpleNamespace(**dict(zip(out_names, results)))


ROW, BOTH, FFN = ((T, D), BF), ((2, T, D), BF), ((2, T, FF), BF)
ROW32, TRIPLE = ((T, D), F32), ((T, 3 * D), BF)
RSTD, RSTDS = ((T, WIN), F32), ((2, T, WIN), F32)
PROBS, VEC, MEMKV = ((SENTS, WIN, 2 * T), BF), ((16, D), F32), ((T + 16, 2 * D), BF)
W_IN, W_OUT, W_QKV, W_CROSS, W_SQUARE = ((D, FF), BF), ((FF, D), BF), ((D, 3 * D), BF), ((D, 2 * D), BF), ((D, D), BF)


def twice(kind):
    return ((2,) + kind[0], kind[1])


def at_hand(w):
    return types.SimpleNamespace(**{n: (a, SMEM if n == "lens" else VMEM if a.ndim < 3 or a.shape[1] < 8 else HERE) for n, a in vars(w).items()})


def is_encoder():
    return lax.axis_index("section") == 0


def gains(r):
    return [r.gain[0, j : j + 1, :].astype(F32) for j in range(2)]


def biases(r):
    return [r.bias[0, j : j + 1, :].astype(F32) for j in range(2)]


def first(r):
    enc = is_encoder()
    dec = jnp.logical_not(enc)
    cp = Copies(r.sems)
    load = cp.table(
        x=(r.tok.at[0], r.v_low.at[0]),
        qkv=(r.w_qkv.at[0], r.v_wqkv),
        so=(r.w_so.at[0], r.v_wso),
        fin=(r.w_fin.at[0], r.v_fin),
        fout=(r.w_fout.at[0], r.v_fout),
        cq=(r.w_cross.at[0, :, :D], r.v_cross),
    )
    load.x.start()
    load.qkv.start()
    load.so.start()

    @pl.when(enc)
    def _():
        load.fin.start()
        load.fout.start()

    @pl.when(dec)
    def _():
        load.cq.start()

    prepare(r.lens, r.starts)
    lim = jnp.where(enc, 4 * T, 0)
    r.v_att[...] = jnp.zeros(r.v_att.shape, BF)
    load.x.wait()
    r.v_x[...] = r.v_low[0].astype(F32)
    gain, bias = gains(r), biases(r)
    self_slots, ffn_slots = cp.slots(12), cp.slots(8)

    def self_copies(i):
        pairs = (
            (r.v_qkv, r.qkv), (r.v_probs, r.probs), (r.v_att, r.att), (r.v_xh1, r.xh1), (r.v_rs1, r.rs1),
            (r.v_hlow, r.hlow),
        )
        return [cp.make(a.at[i], b.at[i], self_slots + 2 * n + i) for n, (a, b) in enumerate(pairs)]

    def ffn_copies(i):
        pairs = ((r.v_z, r.z), (r.v_gd, r.gd), (r.v_xh2, r.xh2), (r.v_rs2, r.rs2))
        return [cp.make(a.at[i], b.at[i], ffn_slots + 2 * n + i) for n, (a, b) in enumerate(pairs)]

    @pl.loop(0, REPEATS)
    def _(i):
        @pl.when(i == 0)
        def _():
            load.qkv.wait()
            load.so.wait()

        @pl.when(jnp.logical_or(enc, i == 0))
        def _():
            self_forward(
                r.v_x, r.v_low.at[i], r.v_wqkv, r.v_wso, r.v_qkv.at[i], r.v_att.at[i], r.v_probs.at[i],
                r.v_xh1.at[i], r.v_rs1.at[i], gain[0], bias[0], r.v_h, r.v_hlow.at[i], r.lens, r.starts,
                lax.axis_index("section"), lim,
            )
            for c in self_copies(i):
                c.start()

        @pl.when(jnp.logical_and(enc, i == 0))
        def _():
            load.fin.wait()
            load.fout.wait()

        @pl.when(enc)
        def _():
            ffn_forward(
                r.v_h, r.v_hlow.at[i], r.v_fin, r.b_in, r.v_fout, r.b_out, r.v_z.at[i], r.v_gd.at[i],
                r.v_xh2.at[i], r.v_rs2.at[i], gain[1], bias[1], r.v_x, r.v_low.at[i + 1],
            )
            for c in ffn_copies(i):
                c.start()

    dec_out = cp.table(h=(r.v_h, r.h), cq=(r.v_cq, r.cq))
    enc_out = cp.table(x1=(r.v_low.at[1], r.x1low), mem=(r.v_low.at[2], r.mem))

    @pl.when(dec)
    def _():
        load.cq.wait()
        r.v_cq[...] = nn(r.v_hlow[0], r.v_cross[...]).astype(BF)
        for c in every(dec_out):
            c.start()
        for c in self_copies(0) + every(dec_out):
            c.wait()

    @pl.when(enc)
    def _():
        for c in every(enc_out):
            c.start()
        for i in range(REPEATS):
            for c in self_copies(i) + ffn_copies(i):
                c.wait()
        for c in every(enc_out):
            c.wait()


def first_phase(w):
    saved = dict(
        qkv=twice(TRIPLE), probs=twice(PROBS), att=BOTH, xh1=BOTH, rs1=RSTDS, hlow=BOTH, z=FFN, gd=FFN, xh2=BOTH,
        rs2=RSTDS, h=ROW32, cq=ROW,
    )
    scratch = dict(saved, low=((3, T, D), BF), wqkv=W_QKV, wso=W_SQUARE, fin=W_IN, fout=W_OUT, cross=W_SQUARE, x=ROW32)
    ins = dict(
        lens=w.lens, tok=w.tok, w_qkv=w.w_qkv, w_so=w.w_so, w_fin=w.w_fin, w_fout=w.w_fout, w_cross=w.w_cross,
        b_in=w.b_in, b_out=w.b_out, gain=w.gain, bias=w.bias,
    )
    return phase(first, ins, dict(saved, x1low=ROW, mem=ROW), scratch, 16 * 10**9)


def middle(r):
    @pl.when(jnp.logical_not(is_encoder()))
    def _():
        cp = Copies(r.sems)
        load = cp.table(
            cq=(r.cq, r.v_cq.at[0]),
            h=(r.h, r.v_h),
            cross=(r.w_cross.at[0], r.v_cross),
            fin=(r.w_fin.at[0], r.v_fin),
            fout=(r.w_fout.at[0], r.v_fout),
            qkv=(r.w_qkv.at[0], r.v_wqkv),
            so=(r.w_so.at[0], r.v_wso),
            og=(r.og, r.v_og),
        )
        for c in every(load):
            c.start()
        prepare(r.lens, r.starts)
        gain, bias = gains(r), biases(r)
        cgain, cbias = r.cgain[...].astype(F32), r.cbias[...].astype(F32)
        for ref in (r.v_vec, r.v_gkv, r.v_catt, r.v_att1, r.v_dcq, r.v_dqkv1):
            ref[...] = jnp.zeros(ref.shape, ref.dtype)
        for c in range(2):
            cols = slice(c * D, (c + 1) * D)
            r.v_mkv[:, cols] = nn(r.mem[...], r.w_c0[0, :, cols]).astype(BF)
        load.cq.wait()
        load.h.wait()
        load.cross.wait()
        saved = (
            (r.v_h1low1, r.h1low1), (r.v_x1low, r.x1low), (r.v_att1, r.att1), (r.v_h2low, r.h2low),
            (r.v_catt, r.catt), (r.v_z, r.z), (r.v_declow, r.decoded),
        )
        early = [cp.make(a, b) for a, b in saved]

        @pl.loop(0, REPEATS)
        def _(i):
            @pl.when(i == 1)
            def _():
                load.qkv.wait()
                load.so.wait()
                self_forward(
                    r.v_x, r.v_x1low, r.v_wqkv, r.v_wso, r.v_qkv1, r.v_att1, r.v_probs1, r.v_xh1, r.v_rs1,
                    gain[0], bias[0], r.v_h, r.v_h1low1, r.lens, r.starts, 1, 0,
                )
                r.v_cq[1] = nn(r.v_h1low1[...], r.v_cross[:, :D]).astype(BF)

            attend(
                r.v_cq.at[i], 0, r.v_mkv, 0, r.v_mkv, D, r.v_catt.at[i], r.v_probsc.at[i], r.lens, r.starts, 1, 0,
                None,
            )
            for rows in chunks():
                v = r.v_h[rows, :] + nn(r.v_catt.at[i][rows, :], r.v_cross[:, D:])
                norm_out(v, rows, r.v_xhc.at[i], r.v_rsc.at[i], cgain, cbias, r.v_h2, r.v_h2low.at[i])

            @pl.when(i == 0)
            def _():
                load.fin.wait()
                load.fout.wait()

            ffn_forward(
                r.v_h2, r.v_h2low.at[i], r.v_fin, r.b_in, r.v_fout, r.b_out, r.v_z.at[i], r.v_gdu.at[i],
                r.v_xh2.at[i], r.v_rs2.at[i], gain[1], bias[1], r.v_x, r.v_declow,
            )

            @pl.when(i == 0)
            def _():
                r.v_x1low[...] = r.v_declow[...]

        for c in early:
            c.start()
        load.og.wait()
        r.v_x[...] = r.v_og[...].astype(F32)

        @pl.loop(0, REPEATS)
        def _(j):
            i = 1 - j
            ffn_backward(
                r.v_x, r.v_xh2.at[i], r.v_rs2.at[i], gain[1], r.v_vec, r.v_dz.at[i], r.v_gdu.at[i], r.v_fin, r.v_fout
            )
            norm_backward(r.v_x, r.v_xhc.at[i], r.v_rsc.at[i], cgain, r.v_dc.at[i], r.v_vec, 9, 10)
            r.v_tmp[...] = nt(r.v_dc[i], r.v_cross[:, D:]).astype(BF)
            attend_backward(
                r.v_cq.at[i], 0, r.v_mkv, 0, r.v_mkv, D, r.v_probsc.at[i], r.v_tmp, (r.v_dcq.at[i], 0),
                (r.v_gkv, 0, D, True), r.lens, r.starts, 1, 0,
            )

            @pl.when(i == 1)
            def _():
                for rows in chunks():
                    r.v_x[rows, :] += nt(r.v_dcq.at[i][rows, :], r.v_cross[:, :D])
                self_backward(
                    r.v_x, r.v_xh1, r.v_rs1, gain[0], r.v_vec, r.v_da1, r.v_wso, r.v_tmp, r.v_qkv1, r.v_probs1,
                    r.v_dqkv1, r.v_wqkv, r.lens, r.starts, 1,
                )

        r.v_gkvlow[:T, :] = r.v_gkv[...].astype(BF)
        r.v_gkvlow[T:, :] = jnp.concatenate(
            [jnp.concatenate([r.v_vec[9:10, :], r.v_vec[10:11, :]], 1), jnp.zeros((15, 2 * D), F32)], 0
        ).astype(BF)
        r.v_gmem[...] = nt(r.v_gkvlow[:T, :], r.w_c0[0]).astype(BF)
        saved = (
            (r.v_gmem, r.gmem), (r.v_gkvlow, r.gkv), (r.v_gdu, r.du), (r.v_dz, r.dz), (r.v_dc, r.dc),
            (r.v_dcq, r.dcq), (r.v_da1, r.da1), (r.v_dqkv1, r.dqkv1), (r.v_x, r.dh), (r.v_vec, r.vec),
        )
        late = [cp.make(a, b) for a, b in saved]
        for c in late:
            c.start()
        for c in early + late:
            c.wait()


def middle_phase(w, one, mem, w_c0):
    outs = dict(
        gmem=ROW, gkv=MEMKV, decoded=ROW, z=FFN, du=FFN, h2low=BOTH, catt=BOTH, h1low1=ROW, dz=BOTH, dc=BOTH, dcq=BOTH,
        att1=ROW, x1low=ROW, da1=ROW, dqkv1=TRIPLE, dh=ROW32, vec=VEC,
    )
    scratch = dict(
        cq=BOTH, h=ROW32, cross=W_CROSS, fin=W_IN, fout=W_OUT, wqkv=W_QKV, wso=W_SQUARE, og=ROW, vec=VEC,
        gkv=((T, 2 * D), F32), catt=BOTH, att1=ROW, dcq=BOTH, dqkv1=TRIPLE, mkv=((T, 2 * D), BF), h1low1=ROW,
        x1low=ROW, h2low=BOTH, z=FFN, declow=ROW, x=ROW32, qkv1=TRIPLE, probs1=PROBS, xh1=ROW, rs1=RSTD,
        probsc=twice(PROBS), xhc=BOTH, rsc=RSTDS, h2=ROW32, gdu=FFN, xh2=BOTH, rs2=RSTDS, dz=BOTH, dc=BOTH, tmp=ROW,
        da1=ROW, gkvlow=MEMKV, gmem=ROW,
    )
    ins = dict(
        lens=w.lens, mem=(mem, VMEM), w_c0=(w_c0, VMEM), cq=(one.cq, HERE), h=(one.h, HERE), og=(w.og[0], HERE),
        w_qkv=w.w_qkv, w_so=w.w_so, w_fin=w.w_fin, w_fout=w.w_fout, w_cross=w.w_cross, b_in=w.b_in, b_out=w.b_out,
        gain=w.gain, bias=w.bias, cgain=w.cgain, cbias=w.cbias,
    )
    return phase(middle, ins, outs, scratch, 30 * 10**9)


PIECES = 16
X_FIRST, Z_FIRST = (0, 1, 2, 3), (0, 2, 3, 1)
ROWS_A = ROWS_B = 512
ROWS_C, ROWS_Q = 32 * 12 + 16, 32 * 12


def place_of(piece, order):
    relative = piece ^ (lax.axis_index("dp") % PIECES)
    place = jnp.int32(0)
    for n, bit in enumerate(order):
        place = place + ((relative >> bit) & 1) * (1 << (3 - n))
    return place


def piece_at(place, order):
    relative = 0
    for n, bit in enumerate(order):
        relative += ((place >> (3 - n)) & 1) << bit
    return relative ^ (lax.axis_index("dp") % PIECES)


def put(dst, order, block, first_row, first_col, high):
    height, width = block.shape
    for j in range(0, height, high):
        place = place_of((first_row + j) // high, order)
        for c in range(0, width, WIN):
            at = ((first_col + c) // WIN) * high
            dst[place, at : at + high, :] = block[j : j + high, c : c + WIN].astype(BF)


def split_out(cp, ref, keep, send):
    made = [cp.make(ref.at[:8], keep), cp.make(ref.at[8:], send)]
    for c in made:
        c.start()
    return made


def third(r):
    enc = is_encoder()
    cp = Copies(r.sems)
    load = cp.table(
        xh2=(r.xh2, r.v_xh2),
        rs2=(r.rs2, r.v_rs2),
        fout=(r.w_fout.at[0], r.v_fout),
        gd=(r.gd, r.v_gdu),
        fin=(r.w_fin.at[0], r.v_fin),
        xh1=(r.xh1.at[1], r.v_xh1),
        rs1=(r.rs1.at[1], r.v_rs1),
        so=(r.w_so.at[0], r.v_wso),
        qkv=(r.qkv.at[1], r.v_qkv1),
        probs=(r.probs.at[1], r.v_probs1),
        wqkv=(r.w_qkv.at[0], r.v_wqkv),
        z=(r.z, r.v_z),
        hlow=(r.hlow, r.v_hlow),
    )
    saved = ((r.v_x, r.dh), (r.v_da1, r.da1), (r.v_dqkv1, r.dqkv1), (r.v_vec, r.vec))
    out = [cp.make(a, b) for a, b in saved]

    @pl.when(enc)
    def _():
        for c in every(load):
            c.start()
        prepare(r.lens, r.starts)
        gain = gains(r)
        r.v_vec[...] = jnp.zeros(r.v_vec.shape, F32)
        r.v_dqkv1[...] = jnp.zeros(r.v_dqkv1.shape, BF)
        r.v_x[...] = r.gmem[...].astype(F32)
        for c in (load.xh2, load.rs2, load.fout, load.gd, load.fin):
            c.wait()

        @pl.loop(0, REPEATS)
        def _(j):
            i = 1 - j
            ffn_backward(
                r.v_x, r.v_xh2.at[i], r.v_rs2.at[i], gain[1], r.v_vec, r.v_dz.at[i], r.v_gdu.at[i], r.v_fin, r.v_fout
            )

            @pl.when(i == 1)
            def _():
                for c in (load.xh1, load.rs1, load.so, load.qkv, load.probs, load.wqkv):
                    c.wait()
                self_backward(
                    r.v_x, r.v_xh1, r.v_rs1, gain[0], r.v_vec, r.v_da1, r.v_wso, r.v_tmp, r.v_qkv1, r.v_probs1,
                    r.v_dqkv1, r.v_wqkv, r.lens, r.starts, 0,
                )

        for c in out:
            c.start()
        load.z.wait()
        load.hlow.wait()

    dec_load = cp.table(z=(r.z_d, r.v_z), du=(r.du_d, r.v_gdu), h=(r.h2low_d, r.v_hlow), dz=(r.dz_d, r.v_dz))

    @pl.when(jnp.logical_not(enc))
    def _():
        for c in every(dec_load):
            c.start()
        for c in every(dec_load):
            c.wait()

    hidden, grad_out = rows_of(r.v_hlow), rows_of(r.v_dz)
    for c in range(4):
        cols = slice(c * D, (c + 1) * D)
        put(r.v_a, X_FIRST, tn(hidden, r.v_gdu[:, :, cols].reshape(2 * T, D)), 0, c * D, 32)
    sends = split_out(cp, r.v_a, r.a_keep, r.a_send)
    for c in range(4):
        cols = slice(c * D, (c + 1) * D)
        put(r.v_b, Z_FIRST, tn(r.v_z[:, :, cols].reshape(2 * T, D), grad_out), c * D, 0, 128)
    sends += split_out(cp, r.v_b, r.b_keep, r.b_send)
    for c in sends:
        c.wait()

    @pl.when(enc)
    def _():
        for c in out:
            c.wait()


def third_phase(w, one, two, gmem):
    half_a, half_b = ((8, ROWS_A, WIN), BF), ((8, ROWS_B, WIN), BF)
    outs = dict(dh=ROW32, da1=ROW, dqkv1=TRIPLE, vec=VEC, a_keep=half_a, a_send=half_a, b_keep=half_b, b_send=half_b)
    scratch = dict(
        xh2=BOTH, rs2=RSTDS, fout=W_OUT, gdu=FFN, fin=W_IN, xh1=ROW, rs1=RSTD, wso=W_SQUARE, qkv1=TRIPLE, probs1=PROBS,
        wqkv=W_QKV, z=FFN, hlow=BOTH, x=ROW32, da1=ROW, dqkv1=TRIPLE, vec=VEC, dz=BOTH, tmp=ROW,
        a=((PIECES, ROWS_A, WIN), BF), b=((PIECES, ROWS_B, WIN), BF),
    )
    ins = dict(lens=w.lens, gmem=(gmem, VMEM), w_qkv=w.w_qkv, w_so=w.w_so, w_fin=w.w_fin, w_fout=w.w_fout, gain=w.gain)
    more = dict(
        xh2=one.xh2, rs2=one.rs2, gd=one.gd, xh1=one.xh1, rs1=one.rs1, qkv=one.qkv, probs=one.probs, z=one.z,
        hlow=one.hlow, z_d=two.z, du_d=two.du, h2low_d=two.h2low, dz_d=two.dz,
    )
    ins.update({n: (a, HERE) for n, a in more.items()})
    return phase(third, ins, outs, scratch, 25 * 10**9)


def fourth(r):
    enc = is_encoder()
    dec = jnp.logical_not(enc)
    cp = Copies(r.sems)
    first_slot = cp.slots(6)

    def own(encoder):
        pairs = (
            (r.dh_e if encoder else r.dh_d, r.v_x),
            (r.vec_e if encoder else r.vec_d, r.v_vec),
            (r.da1_e if encoder else r.da1_d, r.v_da.at[1]),
            (r.att.at[1] if encoder else r.att1_d, r.v_att.at[1]),
        )
        return [cp.make(a, b, first_slot + n) for n, (a, b) in enumerate(pairs)]

    load = cp.table(
        xh1=(r.xh1.at[0], r.v_xh1),
        rs1=(r.rs1.at[0], r.v_rs1),
        att=(r.att.at[0], r.v_att.at[0]),
    )
    enc_cross = cp.table(mem=(r.mem, r.v_one.at[0]))
    dec_cross = cp.table(
        cross=(r.w_cross.at[0, :, :D], r.v_cross),
        h0=(r.hlow.at[0], r.v_one.at[0]),
        h1=(r.h1low1, r.v_one.at[1]),
        att=(r.catt, r.v_two),
        dc=(r.dc, r.v_dc),
        dcq=(r.dcq, r.v_dcq),
        layer=(r.decoded, r.v_layer),
    )
    gain = gains(r)

    @pl.when(enc)
    def _():
        for c in own(True) + every(enc_cross):
            c.start()

    @pl.when(dec)
    def _():
        for c in own(False) + every(dec_cross):
            c.start()

    for c in every(load):
        c.start()
    for c in own(True) + every(load):
        c.wait()

    @pl.when(dec)
    def _():
        dec_cross.cross.wait()
        dec_cross.dcq.wait()
        for rows in chunks():
            r.v_x[rows, :] += nt(r.v_dcq.at[0][rows, :], r.v_cross[...])

    norm_backward(r.v_x, r.v_xh1, r.v_rs1, gain[0], r.v_da.at[0], r.v_vec, 5, 7)
    out = cp.table(x=(r.v_x, r.ds), da=(r.v_da.at[0], r.da0))
    for c in every(out):
        c.start()
    layer_slot = cp.slots()
    enc_layer = cp.make(r.v_one.at[0], r.layer.at[0], layer_slot)
    dec_layer = cp.make(r.v_layer, r.layer.at[0], layer_slot)
    put(r.v_c, Z_FIRST, tn(rows_of(r.v_att), rows_of(r.v_da)), 0, 0, 32)

    @pl.when(enc)
    def _():
        enc_cross.mem.wait()
        enc_layer.start()
        for c in range(2):
            cols = slice(c * D, (c + 1) * D)
            put(r.v_c, Z_FIRST, tn(r.v_one[0], r.gkv[:T, cols]), 0, D + c * D, 32)
        tail = r.gkv[T:, :].astype(F32)
        r.v_vec[9:10, :] = tail[0:1, :D]
        r.v_vec[10:11, :] = tail[0:1, D:]

    @pl.when(dec)
    def _():
        dec_cross.layer.wait()
        dec_layer.start()
        for c in (dec_cross.h0, dec_cross.h1, dec_cross.att, dec_cross.dc):
            c.wait()
        put(r.v_c, Z_FIRST, tn(rows_of(r.v_one), rows_of(r.v_dcq)), 0, D, 32)
        put(r.v_c, Z_FIRST, tn(rows_of(r.v_two), rows_of(r.v_dc)), 0, 2 * D, 32)

    for p in range(PIECES):
        line = r.v_vec[p : p + 1, :]
        tile = [line[:, j * WIN : (j + 1) * WIN] for j in range(4)] + [jnp.zeros((12, WIN), F32)]
        r.v_c[place_of(p, Z_FIRST), ROWS_C - 16 :, :] = jnp.concatenate(tile, 0).astype(BF)
    for c in split_out(cp, r.v_c, r.c_keep, r.c_send) + every(out) + [enc_layer]:
        c.wait()


def fourth_phase(w, one, two, three, gkv):
    half_c = ((8, ROWS_C, WIN), BF)
    outs = dict(layer=((1, T, D), BF), ds=ROW32, da0=ROW, c_keep=half_c, c_send=half_c)
    scratch = dict(
        xh1=ROW, rs1=RSTD, att=BOTH, x=ROW32, vec=VEC, da=BOTH, one=BOTH, two=BOTH, dc=BOTH, dcq=BOTH, cross=W_SQUARE,
        layer=ROW, c=((PIECES, ROWS_C, WIN), BF),
    )
    ins = dict(gkv=(gkv, VMEM), gain=w.gain, w_cross=w.w_cross)
    more = dict(
        xh1=one.xh1, rs1=one.rs1, att=one.att, mem=one.mem, hlow=one.hlow, dh_e=three.dh, vec_e=three.vec,
        da1_e=three.da1, dh_d=two.dh, vec_d=two.vec, da1_d=two.da1, att1_d=two.att1, h1low1=two.h1low1, catt=two.catt,
        dc=two.dc, dcq=two.dcq, decoded=two.decoded,
    )
    ins.update({n: (a, HERE) for n, a in more.items()})
    return phase(fourth, ins, outs, scratch, 4 * 10**9)


def fifth(r):
    enc = is_encoder()
    cp = Copies(r.sems)
    first_slot = cp.slots(2)

    def own(encoder):
        pairs = (
            (r.dqkv1_e if encoder else r.dqkv1_d, r.v_dqkv.at[1]),
            (r.x1low_e if encoder else r.x1low_d, r.v_low.at[1]),
        )
        return [cp.make(a, b, first_slot + n) for n, (a, b) in enumerate(pairs)]

    load = cp.table(
        da=(r.da0, r.v_da),
        so=(r.w_so.at[0], r.v_wso),
        qkv=(r.qkv.at[0], r.v_qkv),
        probs=(r.probs.at[0], r.v_probs),
        x=(r.ds, r.v_x),
        wqkv=(r.w_qkv.at[0], r.v_wqkv),
        low=(r.tok.at[0], r.v_low.at[0]),
    )
    for c in every(load):
        c.start()

    @pl.when(enc)
    def _():
        for c in own(True):
            c.start()

    @pl.when(jnp.logical_not(enc))
    def _():
        for c in own(False):
            c.start()

    prepare(r.lens, r.starts)
    r.v_dqkv[0] = jnp.zeros(r.v_dqkv.shape[1:], BF)
    for c in every(load) + own(True):
        c.wait()
    self_tail(
        r.v_x, r.v_da, r.v_wso, r.v_tmp, r.v_qkv, r.v_probs, r.v_dqkv.at[0], r.v_wqkv, r.lens, r.starts,
        lax.axis_index("section"),
    )
    made = [cp.make(r.v_x, r.rows.at[0])]
    made[0].start()
    inputs, grads = rows_of(r.v_low), rows_of(r.v_dqkv)
    for c in range(3):
        cols = slice(c * D, (c + 1) * D)
        put(r.v_q, X_FIRST, tn(inputs, grads[:, cols]), 0, c * D, 32)
    for c in made + split_out(cp, r.v_q, r.q_keep, r.q_send):
        c.wait()


def fifth_phase(w, one, two, three, four, before):
    half_q = ((8, ROWS_Q, WIN), BF)
    outs = dict(rows=((1, T, D), F32), q_keep=half_q, q_send=half_q)
    scratch = dict(
        wso=W_SQUARE, qkv=TRIPLE, probs=PROBS, wqkv=W_QKV, low=BOTH, x=ROW32, da=ROW, dqkv=twice(TRIPLE), tmp=ROW,
        q=((PIECES, ROWS_Q, WIN), BF),
    )
    ins = dict(lens=w.lens, tok=w.tok, w_qkv=w.w_qkv, w_so=w.w_so)
    more = dict(
        qkv=one.qkv, probs=one.probs, x1low_e=one.x1low, x1low_d=two.x1low, dqkv1_e=three.dqkv1, dqkv1_d=two.dqkv1,
        ds=four.ds, da0=four.da0,
    )
    ins.update({n: (a, HERE) for n, a in more.items()})
    ins.update({"before%d" % n: (a, VMEM) for n, a in enumerate(before)})
    return phase(fifth, ins, outs, scratch, 8 * 10**9)


def across(value, bit):
    pairs = [(i, i ^ (1 << bit)) for i in range(lax.axis_size("dp"))]
    return lax.ppermute(value, "dp", pairs)


def added(a, b):
    return (a.astype(F32) + b.astype(F32)).astype(BF)


def halve(keep, send, bit):
    got = across(send, bit)
    half = keep.shape[0] // 2
    if half == 0:
        return added(keep, got), None
    return added(keep[:half], got[:half]), added(keep[half:], got[half:])


def scatter_rest(keep, send, order):
    for bit in order[1:]:
        keep, send = halve(keep, send, bit)
    bit = len(order)
    while (1 << bit) < lax.axis_size("dp"):
        keep = added(keep, across(keep, bit))
        bit += 1
    return keep


def gather(piece, order):
    for bit in reversed(order[1:]):
        piece = jnp.concatenate([piece, across(piece, bit)], 0)
    return piece, across(piece, order[0])


def unpack(kernel, ins, scratch, outs):
    return pl.pallas_call(
        kernel,
        name=kernel.__name__,
        in_specs=[pl.BlockSpec(memory_space=VMEM)] * len(ins),
        out_specs=[pl.BlockSpec(memory_space=HERE if big else VMEM) for _, big in outs],
        out_shape=[jax.ShapeDtypeStruct(s, F32) for s, _ in outs],
        scratch_shapes=[VMEM(s, F32) for s in scratch] + [pltpu.SemaphoreType.DMA((len(scratch), PIECES))],
        compiler_params=pltpu.CompilerParams(vmem_limit_bytes=VMEM_LIMIT),
        cost_estimate=pl.CostEstimate(flops=4 * 10**9, bytes_accessed=12 * 10**6, transcendentals=0),
    )(*ins)


def pieces_out(halves, order, high, first, wide, out, whole, sems):
    made = []
    for place in range(PIECES):
        ref, at = halves[place // 8], place % 8
        rows = pl.ds(pl.multiple_of(piece_at(place, order) * high, high), high)
        for c in range(wide // WIN):
            start = first + c * high
            whole[rows, c * WIN : (c + 1) * WIN] = ref[at, start : start + high, :].astype(F32)
        made.append(pltpu.make_async_copy(whole.at[rows, :], out.at[0, rows, :], sems.at[place]))
        made[-1].start()
    return made


def unpack_in(a0, a1, fin, v_fin, sems):
    for c in pieces_out((a0, a1), X_FIRST, 32, 0, FF, fin, v_fin, sems.at[0]):
        c.wait()


def unpack_out(b0, b1, fout, v_fout, sems):
    for c in pieces_out((b0, b1), Z_FIRST, 128, 0, D, fout, v_fout, sems.at[0]):
        c.wait()


def unpack_qkv(q0, q1, qkv, v_qkv, sems):
    for c in pieces_out((q0, q1), X_FIRST, 32, 0, 3 * D, qkv, v_qkv, sems.at[0]):
        c.wait()


def unpack_rest(c0, c1, so, cross, b_in, b_out, gain, bias, cgain, cbias, v_so, v_cross, sems):
    made = pieces_out((c0, c1), Z_FIRST, 32, 0, D, so, v_so, sems.at[0])
    made += pieces_out((c0, c1), Z_FIRST, 32, 4 * 32, 2 * D, cross, v_cross, sems.at[1])

    def line(p):
        place = place_of(p, Z_FIRST)
        at = place % 8
        tail = jnp.where(place < 8, c0[at, ROWS_C - 16 :, :].astype(F32), c1[at, ROWS_C - 16 :, :].astype(F32))
        return jnp.concatenate([tail[j : j + 1, :] for j in range(4)], 1)

    for n in range(4):
        b_in[:, n * D : (n + 1) * D] = line(n)
    b_out[...] = line(4)
    for n in range(2):
        gain[0, n : n + 1, :] = line(5 + n)
        bias[0, n : n + 1, :] = line(7 + n)
    cgain[...] = line(9)
    cbias[...] = line(10)
    for c in made:
        c.wait()


def body(
    token_rows, lengths, self_qkv, self_out, ffn_in, ffn_in_bias, ffn_out, ffn_out_bias, norm_gain, norm_bias,
    cross_weights, cross_gain, cross_bias, output_grad,
):
    to_decoder, to_encoder = [(0, 1)], [(1, 0)]
    w = at_hand(
        types.SimpleNamespace(
            tok=token_rows, lens=lengths, w_qkv=self_qkv, w_so=self_out, w_fin=ffn_in, b_in=ffn_in_bias, w_fout=ffn_out,
            b_out=ffn_out_bias, gain=norm_gain, bias=norm_bias, w_cross=cross_weights, cgain=cross_gain.reshape(1, D),
            cbias=cross_bias.reshape(1, D), og=output_grad,
        )
    )
    w_c0 = lax.ppermute(cross_weights, "section", to_decoder)
    one = first_phase(w)
    mem = lax.ppermute(one.mem, "section", to_decoder)
    two = middle_phase(w, one, mem, w_c0)
    gmem = lax.ppermute(two.gmem, "section", to_encoder)
    gkv = lax.ppermute(two.gkv, "section", to_encoder)
    three = third_phase(w, one, two, gmem)
    four = fourth_phase(w, one, two, three, gkv)
    a, a_send = halve(three.a_keep, three.a_send, 0)
    b, b_send = halve(three.b_keep, three.b_send, 0)
    five = fifth_phase(w, one, two, three, four, (a_send, b_send))
    c, c_send = halve(four.c_keep, four.c_send, 0)
    q, q_send = halve(five.q_keep, five.q_send, 0)
    a = scatter_rest(a, a_send, X_FIRST)
    b = scatter_rest(b, b_send, Z_FIRST)
    c = scatter_rest(c, c_send, Z_FIRST)
    q = scatter_rest(q, q_send, X_FIRST)
    (g_fin,) = unpack(unpack_in, gather(a, X_FIRST), [(D, FF)], [((1, D, FF), True)])
    (g_fout,) = unpack(unpack_out, gather(b, Z_FIRST), [(FF, D)], [((1, FF, D), True)])
    (g_qkv,) = unpack(unpack_qkv, gather(q, X_FIRST), [(D, 3 * D)], [((1, D, 3 * D), True)])
    small = [(1, FF), (1, D), (1, 2, D), (1, 2, D), (1, D), (1, D)]
    g_so, g_cross, g_bin, g_bout, g_gain, g_bias, g_cgain, g_cbias = unpack(
        unpack_rest,
        gather(c, Z_FIRST),
        [(D, D), (D, 2 * D)],
        [((1, D, D), True), ((1, D, 2 * D), True)] + [(shape, False) for shape in small],
    )
    return (
        four.layer, five.rows, g_qkv, g_so, g_fin, g_bin, g_fout, g_bout, g_gain, g_bias, g_cross, g_cgain.reshape(D),
        g_cbias.reshape(D),
    )


def solution(mesh):
    by_section = P("section")
    in_specs = (
        P("section", "dp"), P("dp"), by_section, by_section, by_section, by_section, by_section, by_section, by_section,
        by_section, by_section, P(), P(), P("dp"),
    )
    out_specs = (P("section", "dp"), P("section", "dp")) + (by_section,) * 9 + (P(), P())
    return jax.shard_map(body, mesh=mesh, in_specs=in_specs, out_specs=out_specs, check_vma=False)
```

time: 784 us -> 307 us (0.39)
  waiting for transfers between devices: 364 us -> 149 us
  matrix products: 122 us -> 0 us
  blocking collectives: 105 us -> 0 us
  Pallas kernels: 0 us -> 97.2 us
  local copies, waits for them, and re-layouts: 93.3 us -> 5.13 us
  other arithmetic: 66.1 us -> 7.33 us
  starting transfers between devices: 3.59 us -> 41.4 us
  between operations: 14.7 us -> 1.59 us
  loops' own time: 10.7 us -> 0 us
    psum x1 -> x0, waiting for transfers between devices: 156 us -> none  [body(): lax.psum((joined[0], joined[1], joined[2], joined[3], joined[4], joined[5...]
    dot_general x47 -> x0, matrix products: 108 us -> none  [the longest x15 34.9 us: product(): return jnp.dot(former, latter, preferred_element_type=jnp.float32)]
    psum x2 -> x0, blocking collectives: 105 us -> none  [the longest x1 63.4 us: body(): lax.psum((joined[0], joined[1], joined[2], joined[3], joined[4], joined[5...]
    pallas_call x0 -> x9, Pallas kernels: none -> 97.2 us  [the longest x5 82.4 us: phase(): pl.pallas_call(kernel, name=body.__name__, in_specs=[pl.BlockSpec(memory_...]
    ppermute x2 -> x36, waiting for transfers between devices: 207 us -> 149 us  [the longest x32 73.7 us: across(): return lax.ppermute(value, 'dp', pairs)]
    broadcast_in_dim x9 -> x0, other arithmetic: 40.8 us -> none  [the longest x1 10.3 us: body(): totals[4][None]]
    ppermute x2 -> x36, starting transfers between devices: 3.55 us -> 41.4 us  [the longest x32 32.4 us: across(): return lax.ppermute(value, 'dp', pairs)]
    slice x21 -> x0, local copies, waits for them, and re-layouts: 22.9 us -> none  [the longest x4 5.31 us: self_block(): projected[:, 2 * D:]]
  transfers between devices with their start and end apart: 3 -> 36, of which waited for: 3 -> 14; matrix products, arithmetic and copies ran while one was open for 1% -> 3% of each run, Pallas kernels for 0% -> 28%
where the time goes in v1:
time: 307 us; the launch traced here: 302 us
  waiting for transfers between devices  149 us (49%)
  Pallas kernels  97.2 us (32%)
  starting transfers between devices  41.4 us (13%)
  other arithmetic  7.33 us (2%)
  local copies, waits for them, and re-layouts  5.13 us (2%)
    pallas_call x5, Pallas kernels, phase(): pl.pallas_call(kernel, name=body.__name__, in_specs=[pl.BlockSpec(memory_...  82.4 us
    ppermute x32, waiting for transfers between devices, across(): return lax.ppermute(value, 'dp', pairs)  73.7 us
    ppermute x1, waiting for transfers between devices, body(): gmem = lax.ppermute(two.gmem, 'section', to_encoder)  65.2 us
    ppermute x32, starting transfers between devices, across(): return lax.ppermute(value, 'dp', pairs)  32.4 us
    pallas_call x4, Pallas kernels, unpack(): pl.pallas_call(kernel, name=kernel.__name__, in_specs=[pl.BlockSpec(memor...  14.8 us
    ppermute x1, waiting for transfers between devices, body(): mem = lax.ppermute(one.mem, 'section', to_decoder)  10.3 us
    convert_element_type x16, other arithmetic, added(): return (a.astype(F32) + b.astype(F32)).astype(BF)  6.68 us
  transfers between devices with their start and end apart: 36, of which 14 were waited for; matrix products, arithmetic and copies ran while one was open for 3% of the time, Pallas kernels for 28%

profile of v1, /device:TPU:0, one launch (start us, length us, event | category | flops | bytes accessed | tf_op | source)
XLA Modules:
  0.0 301.8 jit_solution(12701251605249084225)
XLA Ops:
  0.7 5.1 %collective-permute-start.1 = (bf16[1,512,1024]{2,1,0:T(8,128)(2,1)}, bf16[1,512,1024]{2,1,0:T(8,128)(2,1)S(1)}, u32[]{:S(2)}, u32[]{:S(2)}) collective-permute-start(bf16[1,512,1024]{2,1,0:T(8,128)(2,1)} %refs_2_.6), channel_id=1, source_target_pairs={{0,16},{1,17},{2,18},{3,19},{4,20},{5,21},{6,22},{7,23},{8,24},{9,... | collective-permute-start | bytes 3145736 | tf_op jit(solution)/shard_map/ppermute | solution.py:967
  5.7 22.8 %first.1 = (bf16[2,512,1536]{2,1,0:T(8,128)(2,1)}, bf16[2,8,128,1024]{3,2,1,0:T(8,128)(2,1)}, bf16[2,512,512]{2,1,0:T(8,128)(2,1)}, bf16[2,512,512]{2,1,0:T(8,12...) custom-call(s32[1,2,8]{2,1,0:T(2,128)} %refs_0_.7, ...), custom_call_target="tpu_custom_call" | custom-call | flops 16000000000 | bytes 7873600 | tf_op jit(solution)/shard_map/first/pallas_call | solution.py:265
  28.6 1.3 collective-permute-start
  31.1 10.3 %collective-permute-done.refs_1_ = bf16[512,512]{1,0:T(8,128)(2,1)S(1)} collective-permute-done((bf16[512,512]{1,0:T(8,128)(2,1)}, bf16[512,512]{1,0:T(8,128)(2,1)S(1)}, u32[]{:S(2)}, u32[]{:S(2)}) %collective-permute-start) | collective-permute-done | bytes 524320 | tf_op jit(solution)/shard_map/ppermute | solution.py:969
  41.4 0.8 copy-done.13
  42.5 10.0 %middle.1 = (bf16[512,512]{1,0:T(8,128)(2,1)}, bf16[528,1024]{1,0:T(8,128)(2,1)}, bf16[512,512]{1,0:T(8,128)(2,1)}, bf16[2,512,2048]{2,1,0:T(8,128)(2,1)}, bf16[...) custom-call(s32[1,2,8]{2,1,0:T(2,128)} %refs_0_.7, ...), custom_call_target="tpu_custom_call" | custom-call | flops 30000001024 | bytes 11021376 | tf_op jit(solution)/shard_map/middle/pallas_call | solution.py:265
  52.5 1.3 collective-permute-start.3
  53.8 1.3 collective-permute-start.2
  55.1 65.2 %collective-permute-done.3.refs_1_ = bf16[512,512]{1,0:T(8,128)(2,1)S(1)} collective-permute-done((bf16[512,512]{1,0:T(8,128)(2,1)}, bf16[512,512]{1,0:T(8,128)(2,1)S(1)}, u32[]{:S(2)}, u32[]{:S(2)}) %collective-permute-start.3) | collective-permute-done | bytes 524320 | tf_op jit(solution)/shard_map/ppermute | solution.py:971
  120.3 0.8 copy-done.14
  121.1 25.6 %third.1 = (f32[512,512]{1,0:T(8,128)}, bf16[512,512]{1,0:T(8,128)(2,1)}, bf16[512,1536]{1,0:T(8,128)(2,1)}, f32[16,512]{1,0:T(8,128)}, bf16[8,512,128]{2,1,0:T(...) custom-call(s32[1,2,8]{2,1,0:T(2,128)} %refs_0_.7, ...), custom_call_target="tpu_custom_call" | custom-call | flops 24999999488 | bytes 37226560 | tf_op jit(solution)/shard_map/third/pallas_call | solution.py:265
  147.3 1.0 copy-done.11
  148.3 7.2 %fourth.1 = (bf16[1,512,512]{2,1,0:T(8,128)(2,1)}, f32[512,512]{1,0:T(8,128)}, bf16[512,512]{1,0:T(8,128)(2,1)}, bf16[8,400,128]{2,1,0:T(8,128)(2,1)}, bf16[8,400,128]{2,1,0:T(8,128)(2,1)}) custom-call(bf16[528,1024]{1,0:T(8,128)(2,1)} %copy-done.11, bf16[1,2,512]{2,1,0:T(2,128)(2,1)} %refs_1_.4, bf16[1,512,1024]{2,1,0:T(8,128)(2,1)} %refs_2_.6, ...), custom_call_target="tpu_custom_call" | custom-call | flops 4000000000 | bytes 14256128 | tf_op jit(solution)/shard_map/fourth/pallas_call | solution.py:265
  155.7 1.0 copy-done.2
  156.7 2.3 add_convert_fusion.1
  159.0 1.5 collective-permute-start.22
  160.5 1.1 add_convert_fusion
  161.6 1.6 collective-permute-start.29
  163.1 16.7 %fifth.1 = (f32[1,512,512]{2,1,0:T(8,128)}, bf16[8,384,128]{2,1,0:T(8,128)(2,1)}, bf16[8,384,128]{2,1,0:T(8,128)(2,1)}) custom-call(s32[1,2,8]{2,1,0:T(2,128)} %refs_0_.7, bf16[1,512,512]{2,1,0:T(8,128)(2,1)} %refs_1_.5, bf16[1,512,1536]{2,1,0:T(8,128)(2,1)} %refs_2_.7, bf16[1,512,512]{2,1,0:T(8,128)(2,1)} %refs_3_.5, ...), custom_call_target="tpu_custom_call" | custom-call | flops 8000000000 | bytes 16777280 | tf_op jit(solution)/shard_map/fifth/pallas_call | solution.py:265
  180.7 1.2 add_convert_fusion.11
  181.9 1.6 collective-permute-start.23
  183.5 1.2 add_convert_fusion.9
  184.7 2.7 collective-permute-start.30
  187.3 10.8 %collective-permute-done.15 = bf16[4,400,128]{2,1,0:T(8,128)(2,1)S(1)} collective-permute-done((bf16[4,400,128]{2,1,0:T(8,128)(2,1)S(1)}, bf16[4,400,128]{2,1,0:T(8,128)(2,1)S(1)}, u32[]{:S(2)}, u32[]{:S(2)}) %collective-permute-start.15) | collective-permute-done | bytes 409632 | tf_op jit(solution)/shard_map/ppermute | solution.py:861
  198.2 0.6 collective-permute-start.16
  198.9 4.6 %collective-permute-done.23 = bf16[2,512,128]{2,1,0:T(8,128)(2,1)S(1)} collective-permute-done((bf16[2,512,128]{2,1,0:T(8,128)(2,1)S(1)}, bf16[2,512,128]{2,1,0:T(8,128)(2,1)S(1)}, u32[]{:S(2)}, u32[]{:S(2)}) %collective-permute-start.23) | collective-permute-done | bytes 262176 | tf_op jit(solution)/shard_map/ppermute | solution.py:861
  204.9 1.6 collective-permute-start.7
  206.5 13.2 %collective-permute-done.24 = bf16[1,512,128]{2,1,0:T(8,128)(2,1)S(1)} collective-permute-done((bf16[1,512,128]{2,1,0:T(8,128)(2,1)S(1)}, bf16[1,512,128]{2,1,0:T(8,128)(2,1)S(1)}, u32[]{:S(2)}, u32[]{:S(2)}) %collective-permute-start.24) | collective-permute-done | bytes 131104 | tf_op jit(solution)/shard_map/ppermute | solution.py:861
  220.6 1.6 collective-permute-start.32
  222.2 3.6 %collective-permute-done.17 = bf16[1,400,128]{2,1,0:T(8,128)(2,1)S(1)} collective-permute-done((bf16[1,400,128]{2,1,0:T(8,128)(2,1)S(1)}, bf16[1,400,128]{2,1,0:T(8,128)(2,1)S(1)}, u32[]{:S(2)}, u32[]{:S(2)}) %collective-permute-start.17) | collective-permute-done | bytes 102432 | tf_op jit(solution)/shard_map/ppermute | solution.py:861
  227.2 1.3 collective-permute-done.32
  228.5 2.8 collective-permute-start.33
  231.6 1.9 collective-permute-start.19
  233.5 12.3 %collective-permute-done.33 = bf16[2,512,128]{2,1,0:T(8,128)(2,1)S(1)} collective-permute-done((bf16[2,512,128]{2,1,0:T(8,128)(2,1)S(1)}, bf16[2,512,128]{2,1,0:T(8,128)(2,1)S(1)}, u32[]{:S(2)}, u32[]{:S(2)}) %collective-permute-start.33) | collective-permute-done | bytes 262176 | tf_op jit(solution)/shard_map/ppermute | solution.py:861
  246.0 5.2 %collective-permute-done.8 = bf16[2,384,128]{2,1,0:T(8,128)(2,1)S(1)} collective-permute-done((bf16[2,384,128]{2,1,0:T(8,128)(2,1)S(1)}, bf16[2,384,128]{2,1,0:T(8,128)(2,1)S(1)}, u32[]{:S(2)}, u32[]{:S(2)}) %collective-permute-start.8) | collective-permute-done | bytes 196640 | tf_op jit(solution)/shard_map/ppermute | solution.py:861
  251.3 1.5 collective-permute-start.20
  252.9 8.7 %collective-permute-done.9 = bf16[1,384,128]{2,1,0:T(8,128)(2,1)S(1)} collective-permute-done((bf16[1,384,128]{2,1,0:T(8,128)(2,1)S(1)}, bf16[1,384,128]{2,1,0:T(8,128)(2,1)S(1)}, u32[]{:S(2)}, u32[]{:S(2)}) %collective-permute-start.9) | collective-permute-done | bytes 98336 | tf_op jit(solution)/shard_map/ppermute | solution.py:861
  261.6 3.4 %collective-permute-start.10 = (bf16[1,384,128]{2,1,0:T(8,128)(2,1)S(1)}, bf16[1,384,128]{2,1,0:T(8,128)(2,1)S(1)}, u32[]{:S(2)}, u32[]{:S(2)}) collective-permute-start(bf16[1,384,128]{2,1,0:T(8,128)(2,1)S(1)} %add_convert_fusion.25), channel_id=1, source_target_pairs={{0,8},{1,9},{2,10},{3,11},{4,12},{5,13},{6,14},{7,15},{8,0},{9,1},... | collective-permute-start | bytes 294920 | tf_op jit(solution)/shard_map/ppermute | solution.py:861
  265.1 1.4 collective-permute-start.27
  266.6 4.2 %collective-permute-done.10 = bf16[1,384,128]{2,1,0:T(8,128)(2,1)S(1)} collective-permute-done((bf16[1,384,128]{2,1,0:T(8,128)(2,1)S(1)}, bf16[1,384,128]{2,1,0:T(8,128)(2,1)S(1)}, u32[]{:S(2)}, u32[]{:S(2)}) %collective-permute-start.10) | collective-permute-done | bytes 98336 | tf_op jit(solution)/shard_map/ppermute | solution.py:861
  270.8 3.2 %collective-permute-start.11 = (bf16[2,384,128]{2,1,0:T(8,128)(2,1)S(1)}, bf16[2,384,128]{2,1,0:T(8,128)(2,1)S(1)}, u32[]{:S(2)}, u32[]{:S(2)}) collective-permute-start(bf16[2,384,128]{2,1,0:T(8,128)(2,1)S(1)} %pad_maximum_fusion.11), channel_id=1, source_target_pairs={{0,4},{1,5},{2,6},{3,7},{4,0},{5,1},{6,2},{7,3},{8,12},{9,13},{10,... | collective-permute-start | bytes 589832 | tf_op jit(solution)/shard_map/ppermute | solution.py:861
  274.9 2.8 collective-permute-done.11
  277.7 1.7 collective-permute-start.12
  279.6 6.6 %collective-permute-done.12 = bf16[4,384,128]{2,1,0:T(8,128)(2,1)S(1)} collective-permute-done((bf16[4,384,128]{2,1,0:T(8,128)(2,1)S(1)}, bf16[4,384,128]{2,1,0:T(8,128)(2,1)S(1)}, u32[]{:S(2)}, u32[]{:S(2)}) %collective-permute-start.12) | collective-permute-done | bytes 393248 | tf_op jit(solution)/shard_map/ppermute | solution.py:861
  286.4 4.2 %unpack_rest.1 = (f32[1,512,512]{2,1,0:T(8,128)}, f32[1,512,1024]{2,1,0:T(8,128)}, f32[1,2048]{1,0:T(1,128)}, f32[1,512]{1,0:T(1,128)}, f32[1,2,512]{2,1,0:T(2,1...) custom-call(bf16[8,400,128]{2,1,0:T(8,128)(2,1)} %copy-done.6, ...), custom_call_target="tpu_custom_call" | custom-call | flops 4000000000 | bytes 12000000 | tf_op jit(solution)/shard_map/unpack_rest/pallas_call | solution.py:893
  290.7 3.7 %unpack_out.1 = f32[1,2048,512]{2,1,0:T(8,128)} custom-call(bf16[8,512,128]{2,1,0:T(8,128)(2,1)} %copy-done.3, bf16[8,512,128]{2,1,0:T(8,128)(2,1)} %collective-permute-done.35.b1), custom_call_target="tpu_custom_call" | custom-call | flops 4000000000 | bytes 12000000 | tf_op jit(solution)/shard_map/unpack_out/pallas_call | solution.py:893
  294.4 3.7 %unpack_in.1 = f32[1,512,2048]{2,1,0:T(8,128)} custom-call(bf16[8,512,128]{2,1,0:T(8,128)(2,1)} %copy-done.4, bf16[8,512,128]{2,1,0:T(8,128)(2,1)} %collective-permute-done.28.a1), custom_call_target="tpu_custom_call" | custom-call | flops 4000000000 | bytes 12000000 | tf_op jit(solution)/shard_map/unpack_in/pallas_call | solution.py:893
  298.1 3.2 %unpack_qkv.1 = f32[1,512,1536]{2,1,0:T(8,128)} custom-call(bf16[8,384,128]{2,1,0:T(8,128)(2,1)} %copy-done.7, bf16[8,384,128]{2,1,0:T(8,128)(2,1)} %collective-permute-done.13.q1), custom_call_target="tpu_custom_call" | custom-call | flops 4000000000 | bytes 12000000 | tf_op jit(solution)/shard_map/unpack_qkv/pallas_call | solution.py:893
  (93 shorter events, 8.8 us)
Async XLA Ops:
  0.6 29.3 %copy-start.9 = (bf16[512]{0:T(512)(128)(2,1)S(1)}, bf16[512]{0:T(512)(128)(2,1)}, u32[]{:S(2)}) copy-start(bf16[512]{0:T(512)(128)(2,1)} %param.25) | copy-start | bytes 3076
  0.7 29.8 %copy-start.10 = (bf16[512]{0:T(512)(128)(2,1)S(1)}, bf16[512]{0:T(512)(128)(2,1)}, u32[]{:S(2)}) copy-start(bf16[512]{0:T(512)(128)(2,1)} %param.26) | copy-start | bytes 3076
  0.7 40.7 %collective-permute-start.1 = (bf16[1,512,1024]{2,1,0:T(8,128)(2,1)}, bf16[1,512,1024]{2,1,0:T(8,128)(2,1)S(1)}, u32[]{:S(2)}, u32[]{:S(2)}) collective-permute-start(bf16[1,512,1024]{2,1,0:T(8,128)(2,1)} %refs_2_.6), channel_id=1, source_target_pairs={{0,16},{1,17},{2,18},{3,19},{4,20},{5,21},{6,22},{7,23},{8,24},{9,... | collective-permute-start | bytes 3145736 | tf_op jit(solution)/shard_map/ppermute | solution.py:967
  28.6 12.8 %collective-permute-start = (bf16[512,512]{1,0:T(8,128)(2,1)}, bf16[512,512]{1,0:T(8,128)(2,1)S(1)}, u32[]{:S(2)}, u32[]{:S(2)}) collective-permute-start(bf16[512,512]{1,0:T(8,128)(2,1)} %get-tuple-element.68.refs_6_), channel_id=1, source_target_pairs={{0,16},{1,17},{2,18},{3,19},{4,20},{5,21},{6,22},{7,23},{8,24},{9,... | collective-permute-start | bytes 1572872 | tf_op jit(solution)/shard_map/ppermute | solution.py:969
  41.4 1.2 copy-start.12
  52.5 67.8 %collective-permute-start.3 = (bf16[512,512]{1,0:T(8,128)(2,1)}, bf16[512,512]{1,0:T(8,128)(2,1)S(1)}, u32[]{:S(2)}, u32[]{:S(2)}) collective-permute-start(bf16[512,512]{1,0:T(8,128)(2,1)} %get-tuple-element.76), channel_id=1, source_target_pairs={{16,0},{17,1},{18,2},{19,3},{20,4},{21,5},{22,6},{23,7},{24,8},{25... | collective-permute-start | bytes 1572872 | tf_op jit(solution)/shard_map/ppermute | solution.py:971
  53.8 93.5 %collective-permute-start.2 = (bf16[528,1024]{1,0:T(8,128)(2,1)}, bf16[528,1024]{1,0:T(8,128)(2,1)S(1)}, u32[]{:S(2)}, u32[]{:S(2)}) collective-permute-start(bf16[528,1024]{1,0:T(8,128)(2,1)} %get-tuple-element.71), channel_id=1, source_target_pairs={{16,0},{17,1},{18,2},{19,3},{20,4},{21,5},{22,6},{23,7},{24,8},{25... | collective-permute-start | bytes 3244040 | tf_op jit(solution)/shard_map/ppermute | solution.py:972
  146.8 9.0 %collective-permute-start.4 = (bf16[8,512,128]{2,1,0:T(8,128)(2,1)}, bf16[8,512,128]{2,1,0:T(8,128)(2,1)S(1)}, u32[]{:S(2)}, u32[]{:S(2)}) collective-permute-start(bf16[8,512,128]{2,1,0:T(8,128)(2,1)} %get-tuple-element.107), channel_id=1, source_target_pairs={{0,1},{1,0},{2,3},{3,2},{4,5},{5,4},{6,7},{7,6},{8,9},{9,8},{10,11... | collective-permute-start | bytes 3145736 | tf_op jit(solution)/shard_map/ppermute | solution.py:861
  146.8 13.6 %collective-permute-start.5 = (bf16[8,512,128]{2,1,0:T(8,128)(2,1)}, bf16[8,512,128]{2,1,0:T(8,128)(2,1)S(1)}, u32[]{:S(2)}, u32[]{:S(2)}) collective-permute-start(bf16[8,512,128]{2,1,0:T(8,128)(2,1)} %get-tuple-element.109), channel_id=1, source_target_pairs={{0,1},{1,0},{2,3},{3,2},{4,5},{5,4},{6,7},{7,6},{8,9},{9,8},{10,11... | collective-permute-start | bytes 3145736 | tf_op jit(solution)/shard_map/ppermute | solution.py:861
  147.3 1.0 copy-start.11
  148.3 8.4 %copy-start.1 = (bf16[8,512,128]{2,1,0:T(8,128)(2,1)S(1)}, bf16[8,512,128]{2,1,0:T(8,128)(2,1)}, u32[]{:S(2)}) copy-start(bf16[8,512,128]{2,1,0:T(8,128)(2,1)} %get-tuple-element.106) | copy-start | bytes 3145732
  155.6 4.9 %copy-start = (bf16[8,512,128]{2,1,0:T(8,128)(2,1)S(1)}, bf16[8,512,128]{2,1,0:T(8,128)(2,1)}, u32[]{:S(2)}) copy-start(bf16[8,512,128]{2,1,0:T(8,128)(2,1)} %get-tuple-element.108) | copy-start | bytes 3145732
  155.6 24.3 %collective-permute-start.14 = (bf16[8,400,128]{2,1,0:T(8,128)(2,1)}, bf16[8,400,128]{2,1,0:T(8,128)(2,1)S(1)}, u32[]{:S(2)}, u32[]{:S(2)}) collective-permute-start(bf16[8,400,128]{2,1,0:T(8,128)(2,1)} %get-tuple-element.114), channel_id=1, source_target_pairs={{0,1},{1,0},{2,3},{3,2},{4,5},{5,4},{6,7},{7,6},{8,9},{9,8},{10,11... | collective-permute-start | bytes 2457608 | tf_op jit(solution)/shard_map/ppermute | solution.py:861
  159.0 21.7 %collective-permute-start.22 = (bf16[4,512,128]{2,1,0:T(8,128)(2,1)}, bf16[4,512,128]{2,1,0:T(8,128)(2,1)}, u32[]{:S(2)}, u32[]{:S(2)}) collective-permute-start(bf16[4,512,128]{2,1,0:T(8,128)(2,1)} %get-tuple-element.126.refs_12_), channel_id=1, source_target_pairs={{0,2},{1,3},{2,0},{3,1},{4,6},{5,7},{6,4},{7,5},{8,10},{9,11},{10,... | collective-permute-start | bytes 1572872 | tf_op jit(solution)/shard_map/ppermute | solution.py:861
  161.6 21.9 %collective-permute-start.29 = (bf16[4,512,128]{2,1,0:T(8,128)(2,1)}, bf16[4,512,128]{2,1,0:T(8,128)(2,1)}, u32[]{:S(2)}, u32[]{:S(2)}) collective-permute-start(bf16[4,512,128]{2,1,0:T(8,128)(2,1)} %get-tuple-element.124.refs_13_), channel_id=1, source_target_pairs={{0,4},{1,5},{2,6},{3,7},{4,0},{5,1},{6,2},{7,3},{8,12},{9,13},{10,... | collective-permute-start | bytes 1572872 | tf_op jit(solution)/shard_map/ppermute | solution.py:861
  163.1 16.8 %copy-start.5 = (bf16[8,400,128]{2,1,0:T(8,128)(2,1)S(1)}, bf16[8,400,128]{2,1,0:T(8,128)(2,1)}, u32[]{:S(2)}) copy-start(bf16[8,400,128]{2,1,0:T(8,128)(2,1)} %get-tuple-element.113) | copy-start | bytes 2457604
  179.8 24.9 %collective-permute-start.6 = (bf16[8,384,128]{2,1,0:T(8,128)(2,1)}, bf16[8,384,128]{2,1,0:T(8,128)(2,1)S(1)}, u32[]{:S(2)}, u32[]{:S(2)}) collective-permute-start(bf16[8,384,128]{2,1,0:T(8,128)(2,1)} %get-tuple-element.112), channel_id=1, source_target_pairs={{0,1},{1,0},{2,3},{3,2},{4,5},{5,4},{6,7},{7,6},{8,9},{9,8},{10,11... | collective-permute-start | bytes 2359304 | tf_op jit(solution)/shard_map/ppermute | solution.py:861
  180.2 24.6 %copy-start.8 = (bf16[8,384,128]{2,1,0:T(8,128)(2,1)S(1)}, bf16[8,384,128]{2,1,0:T(8,128)(2,1)}, u32[]{:S(2)}) copy-start(bf16[8,384,128]{2,1,0:T(8,128)(2,1)} %get-tuple-element.111) | copy-start | bytes 2359300
  180.2 17.9 %collective-permute-start.15 = (bf16[4,400,128]{2,1,0:T(8,128)(2,1)S(1)}, bf16[4,400,128]{2,1,0:T(8,128)(2,1)S(1)}, u32[]{:S(2)}, u32[]{:S(2)}) collective-permute-start(bf16[4,400,128]{2,1,0:T(8,128)(2,1)S(1)} %get-tuple-element.128), channel_id=1, source_target_pairs={{0,4},{1,5},{2,6},{3,7},{4,0},{5,1},{6,2},{7,3},{8,12},{9,13},{10,... | collective-permute-start | bytes 1228808 | tf_op jit(solution)/shard_map/ppermute | solution.py:861
  181.9 21.6 %collective-permute-start.23 = (bf16[2,512,128]{2,1,0:T(8,128)(2,1)S(1)}, bf16[2,512,128]{2,1,0:T(8,128)(2,1)S(1)}, u32[]{:S(2)}, u32[]{:S(2)}) collective-permute-start(bf16[2,512,128]{2,1,0:T(8,128)(2,1)S(1)} %get-tuple-element.134), channel_id=1, source_target_pairs={{0,4},{1,5},{2,6},{3,7},{4,0},{5,1},{6,2},{7,3},{8,12},{9,13},{10,... | collective-permute-start | bytes 786440 | tf_op jit(solution)/shard_map/ppermute | solution.py:861
  184.7 19.4 %collective-permute-start.30 = (bf16[2,512,128]{2,1,0:T(8,128)(2,1)S(1)}, bf16[2,512,128]{2,1,0:T(8,128)(2,1)S(1)}, u32[]{:S(2)}, u32[]{:S(2)}) collective-permute-start(bf16[2,512,128]{2,1,0:T(8,128)(2,1)S(1)} %get-tuple-element.132), channel_id=1, source_target_pairs={{0,8},{1,9},{2,10},{3,11},{4,12},{5,13},{6,14},{7,15},{8,0},{9,1},... | collective-permute-start | bytes 786440 | tf_op jit(solution)/shard_map/ppermute | solution.py:861
  198.2 21.7 %collective-permute-start.16 = (bf16[2,400,128]{2,1,0:T(8,128)(2,1)S(1)}, bf16[2,400,128]{2,1,0:T(8,128)(2,1)S(1)}, u32[]{:S(2)}, u32[]{:S(2)}) collective-permute-start(bf16[2,400,128]{2,1,0:T(8,128)(2,1)S(1)} %get-tuple-element.136), channel_id=1, source_target_pairs={{0,8},{1,9},{2,10},{3,11},{4,12},{5,13},{6,14},{7,15},{8,0},{9,1},... | collective-permute-start | bytes 614408 | tf_op jit(solution)/shard_map/ppermute | solution.py:861
  203.5 16.3 %collective-permute-start.24 = (bf16[1,512,128]{2,1,0:T(8,128)(2,1)S(1)}, bf16[1,512,128]{2,1,0:T(8,128)(2,1)S(1)}, u32[]{:S(2)}, u32[]{:S(2)}) collective-permute-start(bf16[1,512,128]{2,1,0:T(8,128)(2,1)S(1)} %add_convert_fusion.20), channel_id=1, source_target_pairs={{0,8},{1,9},{2,10},{3,11},{4,12},{5,13},{6,14},{7,15},{8,0},{9,1},... | collective-permute-start | bytes 393224 | tf_op jit(solution)/shard_map/ppermute | solution.py:861
  204.1 16.4 %collective-permute-start.31 = (bf16[1,512,128]{2,1,0:T(8,128)(2,1)S(1)}, bf16[1,512,128]{2,1,0:T(8,128)(2,1)S(1)}, u32[]{:S(2)}, u32[]{:S(2)}) collective-permute-start(bf16[1,512,128]{2,1,0:T(8,128)(2,1)S(1)} %add_convert_fusion.17), channel_id=1, source_target_pairs={{0,2},{1,3},{2,0},{3,1},{4,6},{5,7},{6,4},{7,5},{8,10},{9,11},{10,... | collective-permute-start | bytes 393224 | tf_op jit(solution)/shard_map/ppermute | solution.py:861
  204.9 26.4 %collective-permute-start.7 = (bf16[4,384,128]{2,1,0:T(8,128)(2,1)S(1)}, bf16[4,384,128]{2,1,0:T(8,128)(2,1)S(1)}, u32[]{:S(2)}, u32[]{:S(2)}) collective-permute-start(bf16[4,384,128]{2,1,0:T(8,128)(2,1)S(1)} %get-tuple-element.130), channel_id=1, source_target_pairs={{0,2},{1,3},{2,0},{3,1},{4,6},{5,7},{6,4},{7,5},{8,10},{9,11},{10,... | collective-permute-start | bytes 1179656 | tf_op jit(solution)/shard_map/ppermute | solution.py:861
  219.8 6.8 %collective-permute-start.25 = (bf16[1,512,128]{2,1,0:T(8,128)(2,1)S(1)}, bf16[1,512,128]{2,1,0:T(8,128)(2,1)S(1)}, u32[]{:S(2)}, u32[]{:S(2)}) collective-permute-start(bf16[1,512,128]{2,1,0:T(8,128)(2,1)S(1)} %add_convert_fusion.19), channel_id=1, source_target_pairs={{0,8},{1,9},{2,10},{3,11},{4,12},{5,13},{6,14},{7,15},{8,0},{9,1},... | collective-permute-start | bytes 393224 | tf_op jit(solution)/shard_map/ppermute | solution.py:861
  219.9 5.8 %collective-permute-start.17 = (bf16[1,400,128]{2,1,0:T(8,128)(2,1)S(1)}, bf16[1,400,128]{2,1,0:T(8,128)(2,1)S(1)}, u32[]{:S(2)}, u32[]{:S(2)}) collective-permute-start(bf16[1,400,128]{2,1,0:T(8,128)(2,1)S(1)} %add_convert_fusion.23), channel_id=1, source_target_pairs={{0,2},{1,3},{2,0},{3,1},{4,6},{5,7},{6,4},{7,5},{8,10},{9,11},{10,... | collective-permute-start | bytes 307208 | tf_op jit(solution)/shard_map/ppermute | solution.py:861
  220.6 7.9 %collective-permute-start.32 = (bf16[1,512,128]{2,1,0:T(8,128)(2,1)S(1)}, bf16[1,512,128]{2,1,0:T(8,128)(2,1)S(1)}, u32[]{:S(2)}, u32[]{:S(2)}) collective-permute-start(bf16[1,512,128]{2,1,0:T(8,128)(2,1)S(1)} %add_convert_fusion.16), channel_id=1, source_target_pairs={{0,2},{1,3},{2,0},{3,1},{4,6},{5,7},{6,4},{7,5},{8,10},{9,11},{10,... | collective-permute-start | bytes 393224 | tf_op jit(solution)/shard_map/ppermute | solution.py:861
  225.8 5.8 %collective-permute-start.18 = (bf16[1,400,128]{2,1,0:T(8,128)(2,1)S(1)}, bf16[1,400,128]{2,1,0:T(8,128)(2,1)S(1)}, u32[]{:S(2)}, u32[]{:S(2)}) collective-permute-start(bf16[1,400,128]{2,1,0:T(8,128)(2,1)S(1)} %add_convert_fusion.22), channel_id=1, source_target_pairs={{0,2},{1,3},{2,0},{3,1},{4,6},{5,7},{6,4},{7,5},{8,10},{9,11},{10,... | collective-permute-start | bytes 307208 | tf_op jit(solution)/shard_map/ppermute | solution.py:861
  226.6 38.5 %collective-permute-start.26 = (bf16[2,512,128]{2,1,0:T(8,128)(2,1)S(1)}, bf16[2,512,128]{2,1,0:T(8,128)(2,1)S(1)}, u32[]{:S(2)}, u32[]{:S(2)}) collective-permute-start(bf16[2,512,128]{2,1,0:T(8,128)(2,1)S(1)} %pad_maximum_fusion.8), channel_id=1, source_target_pairs={{0,4},{1,5},{2,6},{3,7},{4,0},{5,1},{6,2},{7,3},{8,12},{9,13},{10,... | collective-permute-start | bytes 786440 | tf_op jit(solution)/shard_map/ppermute | solution.py:861
  228.5 17.3 %collective-permute-start.33 = (bf16[2,512,128]{2,1,0:T(8,128)(2,1)S(1)}, bf16[2,512,128]{2,1,0:T(8,128)(2,1)S(1)}, u32[]{:S(2)}, u32[]{:S(2)}) collective-permute-start(bf16[2,512,128]{2,1,0:T(8,128)(2,1)S(1)} %pad_maximum_fusion.9), channel_id=1, source_target_pairs={{0,8},{1,9},{2,10},{3,11},{4,12},{5,13},{6,14},{7,15},{8,0},{9,1},... | collective-permute-start | bytes 786440 | tf_op jit(solution)/shard_map/ppermute | solution.py:861
  231.5 19.7 %collective-permute-start.8 = (bf16[2,384,128]{2,1,0:T(8,128)(2,1)S(1)}, bf16[2,384,128]{2,1,0:T(8,128)(2,1)S(1)}, u32[]{:S(2)}, u32[]{:S(2)}) collective-permute-start(bf16[2,384,128]{2,1,0:T(8,128)(2,1)S(1)} %get-tuple-element.138), channel_id=1, source_target_pairs={{0,4},{1,5},{2,6},{3,7},{4,0},{5,1},{6,2},{7,3},{8,12},{9,13},{10,... | collective-permute-start | bytes 589832 | tf_op jit(solution)/shard_map/ppermute | solution.py:861
  231.6 19.7 %collective-permute-start.19 = (bf16[2,400,128]{2,1,0:T(8,128)(2,1)S(1)}, bf16[2,400,128]{2,1,0:T(8,128)(2,1)S(1)}, u32[]{:S(2)}, u32[]{:S(2)}) collective-permute-start(bf16[2,400,128]{2,1,0:T(8,128)(2,1)S(1)} %pad_maximum_fusion.10), channel_id=1, source_target_pairs={{0,8},{1,9},{2,10},{3,11},{4,12},{5,13},{6,14},{7,15},{8,0},{9,1},... | collective-permute-start | bytes 614408 | tf_op jit(solution)/shard_map/ppermute | solution.py:861
  245.9 28.4 %collective-permute-start.34 = (bf16[4,512,128]{2,1,0:T(8,128)(2,1)S(1)}, bf16[4,512,128]{2,1,0:T(8,128)(2,1)S(1)}, u32[]{:S(2)}, u32[]{:S(2)}) collective-permute-start(bf16[4,512,128]{2,1,0:T(8,128)(2,1)S(1)} %pad_maximum_fusion.5), channel_id=1, source_target_pairs={{0,4},{1,5},{2,6},{3,7},{4,0},{5,1},{6,2},{7,3},{8,12},{9,13},{10,... | collective-permute-start | bytes 1572872 | tf_op jit(solution)/shard_map/ppermute | solution.py:861
  251.2 10.4 %collective-permute-start.9 = (bf16[1,384,128]{2,1,0:T(8,128)(2,1)S(1)}, bf16[1,384,128]{2,1,0:T(8,128)(2,1)S(1)}, u32[]{:S(2)}, u32[]{:S(2)}) collective-permute-start(bf16[1,384,128]{2,1,0:T(8,128)(2,1)S(1)} %add_convert_fusion.26), channel_id=1, source_target_pairs={{0,8},{1,9},{2,10},{3,11},{4,12},{5,13},{6,14},{7,15},{8,0},{9,1},... | collective-permute-start | bytes 294920 | tf_op jit(solution)/shard_map/ppermute | solution.py:861
  251.3 22.7 %collective-permute-start.20 = (bf16[4,400,128]{2,1,0:T(8,128)(2,1)S(1)}, bf16[4,400,128]{2,1,0:T(8,128)(2,1)S(1)}, u32[]{:S(2)}, u32[]{:S(2)}) collective-permute-start(bf16[4,400,128]{2,1,0:T(8,128)(2,1)S(1)} %pad_maximum_fusion.6), channel_id=1, source_target_pairs={{0,4},{1,5},{2,6},{3,7},{4,0},{5,1},{6,2},{7,3},{8,12},{9,13},{10,... | collective-permute-start | bytes 1228808 | tf_op jit(solution)/shard_map/ppermute | solution.py:861
  261.6 9.2 %collective-permute-start.10 = (bf16[1,384,128]{2,1,0:T(8,128)(2,1)S(1)}, bf16[1,384,128]{2,1,0:T(8,128)(2,1)S(1)}, u32[]{:S(2)}, u32[]{:S(2)}) collective-permute-start(bf16[1,384,128]{2,1,0:T(8,128)(2,1)S(1)} %add_convert_fusion.25), channel_id=1, source_target_pairs={{0,8},{1,9},{2,10},{3,11},{4,12},{5,13},{6,14},{7,15},{8,0},{9,1},... | collective-permute-start | bytes 294920 | tf_op jit(solution)/shard_map/ppermute | solution.py:861
  265.1 14.3 %collective-permute-start.27 = (bf16[4,512,128]{2,1,0:T(8,128)(2,1)S(1)}, bf16[4,512,128]{2,1,0:T(8,128)(2,1)S(1)}, u32[]{:S(2)}, u32[]{:S(2)}) collective-permute-start(bf16[4,512,128]{2,1,0:T(8,128)(2,1)S(1)} %pad_maximum_fusion.4), channel_id=1, source_target_pairs={{0,2},{1,3},{2,0},{3,1},{4,6},{5,7},{6,4},{7,5},{8,10},{9,11},{10,... | collective-permute-start | bytes 1572872 | tf_op jit(solution)/shard_map/ppermute | solution.py:861
  270.8 6.9 %collective-permute-start.11 = (bf16[2,384,128]{2,1,0:T(8,128)(2,1)S(1)}, bf16[2,384,128]{2,1,0:T(8,128)(2,1)S(1)}, u32[]{:S(2)}, u32[]{:S(2)}) collective-permute-start(bf16[2,384,128]{2,1,0:T(8,128)(2,1)S(1)} %pad_maximum_fusion.11), channel_id=1, source_target_pairs={{0,4},{1,5},{2,6},{3,7},{4,0},{5,1},{6,2},{7,3},{8,12},{9,13},{10,... | collective-permute-start | bytes 589832 | tf_op jit(solution)/shard_map/ppermute | solution.py:861
  274.1 12.2 %copy-start.6 = (bf16[8,400,128]{2,1,0:T(8,128)(2,1)}, bf16[8,400,128]{2,1,0:T(8,128)(2,1)S(1)}, u32[]{:S(2)}) copy-start(bf16[8,400,128]{2,1,0:T(8,128)(2,1)S(1)} %pad_maximum_fusion.2.c0) | copy-start | bytes 2457604
  274.2 12.3 %collective-permute-start.21 = (bf16[8,400,128]{2,1,0:T(8,128)(2,1)S(1)}, bf16[8,400,128]{2,1,0:T(8,128)(2,1)}, u32[]{:S(2)}, u32[]{:S(2)}) collective-permute-start(bf16[8,400,128]{2,1,0:T(8,128)(2,1)S(1)} %pad_maximum_fusion.2.c0), channel_id=1, source_target_pairs={{0,1},{1,0},{2,3},{3,2},{4,5},{5,4},{6,7},{7,6},{8,9},{9,8},{10,11... | collective-permute-start | bytes 2457608 | tf_op jit(solution)/shard_map/ppermute | solution.py:861
  274.4 16.3 %copy-start.3 = (bf16[8,512,128]{2,1,0:T(8,128)(2,1)}, bf16[8,512,128]{2,1,0:T(8,128)(2,1)S(1)}, u32[]{:S(2)}) copy-start(bf16[8,512,128]{2,1,0:T(8,128)(2,1)S(1)} %pad_maximum_fusion.1.b0) | copy-start | bytes 3145732
  274.4 16.3 %collective-permute-start.35 = (bf16[8,512,128]{2,1,0:T(8,128)(2,1)S(1)}, bf16[8,512,128]{2,1,0:T(8,128)(2,1)}, u32[]{:S(2)}, u32[]{:S(2)}) collective-permute-start(bf16[8,512,128]{2,1,0:T(8,128)(2,1)S(1)} %pad_maximum_fusion.1.b0), channel_id=1, source_target_pairs={{0,1},{1,0},{2,3},{3,2},{4,5},{5,4},{6,7},{7,6},{8,9},{9,8},{10,11... | collective-permute-start | bytes 3145736 | tf_op jit(solution)/shard_map/ppermute | solution.py:861
  277.7 8.5 %collective-permute-start.12 = (bf16[4,384,128]{2,1,0:T(8,128)(2,1)S(1)}, bf16[4,384,128]{2,1,0:T(8,128)(2,1)S(1)}, u32[]{:S(2)}, u32[]{:S(2)}) collective-permute-start(bf16[4,384,128]{2,1,0:T(8,128)(2,1)S(1)} %pad_maximum_fusion.7), channel_id=1, source_target_pairs={{0,2},{1,3},{2,0},{3,1},{4,6},{5,7},{6,4},{7,5},{8,10},{9,11},{10,... | collective-permute-start | bytes 1179656 | tf_op jit(solution)/shard_map/ppermute | solution.py:861
  279.5 11.1 %copy-start.4 = (bf16[8,512,128]{2,1,0:T(8,128)(2,1)}, bf16[8,512,128]{2,1,0:T(8,128)(2,1)S(1)}, u32[]{:S(2)}) copy-start(bf16[8,512,128]{2,1,0:T(8,128)(2,1)S(1)} %pad_maximum_fusion.a0) | copy-start | bytes 3145732
  279.6 14.8 %collective-permute-start.28 = (bf16[8,512,128]{2,1,0:T(8,128)(2,1)S(1)}, bf16[8,512,128]{2,1,0:T(8,128)(2,1)}, u32[]{:S(2)}, u32[]{:S(2)}) collective-permute-start(bf16[8,512,128]{2,1,0:T(8,128)(2,1)S(1)} %pad_maximum_fusion.a0), channel_id=1, source_target_pairs={{0,1},{1,0},{2,3},{3,2},{4,5},{5,4},{6,7},{7,6},{8,9},{9,8},{10,11... | collective-permute-start | bytes 3145736 | tf_op jit(solution)/shard_map/ppermute | solution.py:861
  286.3 4.3 %copy-start.7 = (bf16[8,384,128]{2,1,0:T(8,128)(2,1)}, bf16[8,384,128]{2,1,0:T(8,128)(2,1)S(1)}, u32[]{:S(2)}) copy-start(bf16[8,384,128]{2,1,0:T(8,128)(2,1)S(1)} %pad_maximum_fusion.3.q0) | copy-start | bytes 2359300
  286.3 11.8 %collective-permute-start.13 = (bf16[8,384,128]{2,1,0:T(8,128)(2,1)S(1)}, bf16[8,384,128]{2,1,0:T(8,128)(2,1)}, u32[]{:S(2)}, u32[]{:S(2)}) collective-permute-start(bf16[8,384,128]{2,1,0:T(8,128)(2,1)S(1)} %pad_maximum_fusion.3.q0), channel_id=1, source_target_pairs={{0,1},{1,0},{2,3},{3,2},{4,5},{5,4},{6,7},{7,6},{8,9},{9,8},{10,11... | collective-permute-start | bytes 2359304 | tf_op jit(solution)/shard_map/ppermute | solution.py:861
  (3 other events, 2.6 us)
